TPU v7x, 256 devices: a whole 4x4x8 slice. The times are simulated.
256 devices in a mesh: grp: 16 (over y, x), tp: 16 (over z, core).
Axes of the slice: x: 4, y: 4, z: 8, core: 2. Of those that a mesh axis runs over, the one named last changes fastest.
Arguments:
- queries: bfloat16 [512, 128, 576], P(('grp', 'tp')), may hold values from -110 to 110
- latent_cache: bfloat16 [512, 512, 576], P(('grp', 'tp')), may hold values from -6 to 6
- lengths: int32 [512], P(('grp', 'tp')), may hold values from 2 to 512, as said below
- counts: int32 [256], P(('grp', 'tp')), may hold values from 1 to 2, as said below
- residual: bfloat16 [512, 7168], P(None, 'grp'), may hold values from -30 to 30
- value_up: bfloat16 [128, 512, 128], P('tp'), may hold values from -0.75 to 0.75
- out_proj: bfloat16 [16384, 7168], P('tp', 'grp'), may hold values from -0.09375 to 0.09375
- norm_gain: bfloat16 [7168], P('grp'), may hold values from 0.099609375 to 1.8984375
- gate_up: bfloat16 [7168, 2, 18432], P('grp', None, 'tp'), may hold values from -0.0625 to 0.0625
- down_proj: bfloat16 [18432, 7168], P('tp', 'grp'), may hold values from -0.046875 to 0.046875
Outputs:
- mixed: bfloat16 [512, 7168], P('tp', 'grp')
Inputs may be any that keep to these rules, and one draw needn't show every extreme that they name: `lengths`: at least 2; exactly 512 for some slot. `counts`: the slots in use on a device are its first ones; exactly 2 on some device.
All inputs are finite; a program needn't handle non-finite values.
Results may differ from a plain program's by a relative error of at most 0.0065.
Values may be sent and summed in bfloat16 or wider, within the bound.
No kernel may reach another device: no remote copies, remote signals or barrier semaphores. Data moves between devices by JAX's collectives and lax.ppermute only.
A program may use at most 64 MiB of HBM per device.

v0:
```python
import jax
import jax.numpy as jnp
from jax import lax
from jax.sharding import PartitionSpec as P

D = 7168
KL = 512
QKD = 192


def attend_block(queries, cache, lengths, width, start, carry):
    running, totals, accum = carry
    piece = lax.dynamic_slice_in_dim(cache, start, width, 1)
    scores = jnp.einsum(
        "rhk,rlk->rhl", queries, piece, preferred_element_type=jnp.float32
    ) * QKD ** (-0.5)
    place = start + lax.broadcasted_iota(jnp.int32, (1, 1, width), 2)
    scores = jnp.where(place < lengths[:, None, None], scores, -jnp.inf)
    newmax = jnp.maximum(running, jnp.max(scores, axis=2))
    expo = jnp.exp(scores - newmax[:, :, None])
    factor = jnp.exp(running - newmax)
    totals = totals * factor + jnp.sum(expo, axis=2)
    contrib = jnp.einsum(
        "rhl,rlk->rhk",
        expo.astype(jnp.bfloat16),
        piece[:, :, :KL],
        preferred_element_type=jnp.float32,
    )
    accum = accum * factor[:, :, None] + contrib
    return (newmax, totals, accum)


def local(
    queries,
    latent_cache,
    lengths,
    counts,
    residual,
    value_up,
    out_proj,
    norm_gain,
    gate_up,
    down_proj,
):
    slots = queries.shape[0]
    heads = queries.shape[1]
    cache_len = latent_cache.shape[1]
    width = min(256, cache_len)
    in_use = lax.broadcasted_iota(jnp.int32, (slots,), 0) < counts[0]
    initial = (
        jnp.full((slots, heads), -jnp.inf, jnp.float32),
        jnp.zeros((slots, heads), jnp.float32),
        jnp.zeros((slots, heads, KL), jnp.float32),
    )

    def advance(index, carry):
        return attend_block(queries, latent_cache, lengths, width, index * width, carry)

    limit = cache_len // width
    running, totals, accum = lax.fori_loop(0, limit, advance, initial)
    attended = jnp.where(in_use[:, None, None], accum / totals[:, :, None], 0.0).astype(
        jnp.bfloat16
    )
    received = lax.all_to_all(attended, "tp", split_axis=1, concat_axis=0, tiled=True)
    values = jnp.einsum(
        "rhk,hkd->rhd", received, value_up, preferred_element_type=jnp.float32
    ).astype(jnp.bfloat16)
    values = values.reshape(values.shape[0], -1)
    partial_value = jnp.dot(
        lax.all_gather(values, "grp", axis=0, tiled=True),
        out_proj,
        preferred_element_type=jnp.float32,
    )
    all_rows = partial_value.shape[0]
    share = all_rows // lax.axis_size("tp")
    offset = lax.axis_index("tp") * share
    gain = norm_gain.astype(jnp.float32)
    projected = lax.psum(partial_value, "tp")
    combined_all = residual.astype(jnp.float32) + projected
    squares = lax.psum(jnp.sum(combined_all * combined_all, axis=1), "grp")
    normed = (combined_all * lax.rsqrt(squares / D + 1e-06)[:, None] * gain).astype(jnp.bfloat16)
    combined = lax.dynamic_slice_in_dim(combined_all, offset, share, 0)
    joined = gate_up.reshape(gate_up.shape[0], -1)
    units = gate_up.shape[2]
    summed = lax.psum(jnp.dot(normed, joined, preferred_element_type=jnp.float32), "grp")
    hidden = (jax.nn.silu(summed[:, :units]) * summed[:, units:]).astype(jnp.bfloat16)
    terms = jnp.dot(hidden, down_proj, preferred_element_type=jnp.float32)
    mixed = combined + lax.psum_scatter(terms, "tp", scatter_dimension=0, tiled=True)
    return mixed.astype(jnp.bfloat16)


def solution(mesh):
    placed = (
        P(("grp", "tp"), None, None),
        P(("grp", "tp"), None, None),
        P(("grp", "tp")),
        P(("grp", "tp")),
        P(None, "grp"),
        P("tp", None, None),
        P("tp", "grp"),
        P("grp"),
        P("grp", None, "tp"),
        P("tp", "grp"),
    )
    return jax.shard_map(
        local, mesh=mesh, in_specs=placed, out_specs=P("tp", "grp"), check_vma=False
    )
```

profile of v0, /device:TPU:2, one launch (start us, length us, event | category | flops | bytes accessed | tf_op | source)
XLA Modules:
  0.0 427.1 jit_solution(8143189667106468414)
XLA Ops:
  6.5 0.0 copy-start
  6.5 0.0 all-gather.2.cloned.1.call-start
  6.5 7.8 %while.18 = (s32[]{:T(128)}, f32[2,128]{1,0:T(2,128)S(1)}, f32[2,128]{1,0:T(2,128)S(1)}, f32[2,128,512]{2,1,0:T(8,128)S(1)}, s32[2]{0:T(128)}, /*index=5*/bf16[2...) while((s32[]{:T(128)}, f32[2,128]{1,0:T(2,128)S(1)}, ...), condition=%wide.region_3.4_spmd.clone, body=%wide.region_0.3_spmd.clone.sunk | while | flops 143460352 | bytes 3263675 | solution.py:60
  6.5 0.8 broadcast_compare_fusion.2
  7.4 1.6 fusion.41
  9.0 0.1 fusion.43
  9.0 1.4 convolution_add_fusion.2
  10.5 0.7 broadcast_compare_fusion.2
  11.2 1.6 fusion.41
  12.8 0.1 fusion.43
  12.9 1.4 convolution_add_fusion.2
  14.3 0.0 copy-start.4
  14.3 0.1 copy.33
  15.2 0.6 fusion.20
  15.8 19.5 %all_to_all.18 = bf16[2,128,512]{2,0,1:T(2,128)(2,1)S(1)} all-to-all(bf16[2,128,512]{2,0,1:T(2,128)(2,1)S(1)} %fusion.20), channel_id=1, replica_groups=mesh['grp'=16,'tp'=16] {'tp'}, dimensions={1} | all-to-all | bytes 524288 | tf_op jit(solution)/shard_map/all_to_all | solution.py:64
  35.3 0.2 copy.55
  35.5 0.1 all_to_all.16
  35.6 0.0 copy-done
  35.6 0.3 fusion.15
  35.9 0.0 copy-start.1
  35.9 0.6 copy.56
  36.5 0.0 all-gather.2.cloned.1.call-update
  36.6 0.0 all-reduce.3.cloned.1.call-start
  36.6 45.2 %all-gather.2.cloned.1.call-done = bf16[512,1024]{1,0:T(8,128)(2,1)} async-done(((bf16[32,1024]{1,0:T(8,128)(2,1)}), bf16[512,1024]{1,0:T(8,128)(2,1)}) %all-gather.2.cloned.1.call-update) | async-done | bytes 1048592 | tf_op jit(solution)/shard_map/all_gather | solution.py:70
  81.8 0.0 copy-done.4
  81.8 3.0 fusion.23
  84.8 0.0 all-reduce.3.cloned.1.call-update
  84.8 0.0 copy-start.2
  84.8 0.0 all-reduce.5.cloned.1.call-start
  84.9 0.0 copy-done.1
  84.9 1.0 copy.32
  85.9 1.9 copy.47
  87.8 0.0 copy-done.2
  87.8 108.3 %all-reduce.3.cloned.1.call-done = f32[512,448]{1,0:T(8,128)} async-done(((f32[512,448]{1,0:T(8,128)}), f32[512,448]{1,0:T(8,128)}) %all-reduce.3.cloned.1.call-update) | async-done | bytes 917520 | tf_op jit(solution)/shard_map/psum | solution.py:78
  196.1 2.5 multiply_reduce_fusion
  198.6 36.4 %psum.22 = f32[512]{0:T(512)S(1)} all-reduce(f32[512]{0:T(512)S(1)} %get-tuple-element.172), channel_id=1, replica_groups=mesh['grp'=16,'tp'=16] {'grp'}, use_global_device_ids=true, to_apply=%region_6.7 | all-reduce | flops 512 | bytes 4096 | tf_op jit(solution)/shard_map/psum | solution.py:80
  235.0 4.8 %fusion.16 = f32[512,2304]{1,0:T(8,128)} fusion(bf16[448,2304]{1,0:T(8,128)(2,1)S(1)} %bitcast.28, f32[512,448]{1,0:T(8,128)} %get-tuple-element.173, f32[448]{0:T(512)S(1)} %convert_element_type.35, f32[512]{0:T(512)S(1)} %add_rsqrt_fusion), kind=kOutput, calls=%fused_computation.28 | convolution fusion | flops 1057652736 | bytes 7704320 | tf_op jit(solution)/shard_map/dot_general | solution.py:85
  239.8 0.0 copy-start.3
  239.8 0.0 all-reduce.5.cloned.1.call-update
  239.8 0.0 reduce-scatter.4.cloned.1.call-start
  239.9 117.7 %all-reduce.5.cloned.1.call-done = f32[512,2304]{1,0:T(8,128)} async-done(((f32[512,2304]{1,0:T(8,128)}), f32[512,2304]{1,0:T(8,128)}) %all-reduce.5.cloned.1.call-update) | async-done | bytes 4718608 | tf_op jit(solution)/shard_map/psum | solution.py:85
  357.6 0.0 copy-done.3
  357.6 4.3 fusion.13
  361.9 0.0 reduce-scatter.4.cloned.1.call-update
  361.9 57.2 %reduce-scatter.4.cloned.1.call-done = f32[32,448]{1,0:T(8,128)} async-done(((f32[512,448]{1,0:T(8,128)}), f32[32,448]{1,0:T(8,128)}) %reduce-scatter.4.cloned.1.call-update) | async-done | bytes 57360 | tf_op jit(solution)/shard_map/reduce_scatter | solution.py:88
  419.1 1.5 add_convert_fusion
  (14 shorter events, 0.1 us)
Async XLA Ops:
  6.5 29.1 %copy-start = (bf16[8,512,128]{2,1,0:T(8,128)(2,1)S(1)}, bf16[8,512,128]{2,1,0:T(8,128)(2,1)}, u32[]{:S(2)}) copy-start(bf16[8,512,128]{2,1,0:T(8,128)(2,1)} %param.17) | copy-start | bytes 3145732
  6.5 75.3 %all-gather.2.cloned.1.call-start = ((), (), s32[]{:S(2)}) async-start(), calls=%async_computation.2 | async-start | bytes 1114112 | tf_op jit(solution)/shard_map/all_gather | solution.py:70
  14.3 67.5 %copy-start.4 = (bf16[1024,448]{0,1:T(8,128)(2,1)S(1)}, bf16[1024,448]{0,1:T(8,128)(2,1)}, u32[]{:S(2)}) copy-start(bf16[1024,448]{0,1:T(8,128)(2,1)} %param.18) | copy-start | bytes 2752516
  35.9 49.0 %copy-start.1 = (bf16[512,448]{0,1:T(8,128)(2,1)S(1)}, bf16[512,448]{0,1:T(8,128)(2,1)}, u32[]{:S(2)}) copy-start(bf16[512,448]{0,1:T(8,128)(2,1)} %param.16) | copy-start | bytes 1376260
  36.6 159.5 %all-reduce.3.cloned.1.call-start = ((), (), s32[]{:S(2)}) async-start(), calls=%async_computation.3 | async-start | bytes 2097152 | tf_op jit(solution)/shard_map/psum | solution.py:78
  84.8 3.0 copy-start.2
  84.8 272.7 %all-reduce.5.cloned.1.call-start = ((), (), s32[]{:S(2)}) async-start(), calls=%async_computation.4 | async-start | bytes 9437184 | tf_op jit(solution)/shard_map/psum | solution.py:85
  239.8 117.8 %copy-start.3 = (bf16[1152,448]{0,1:T(8,128)(2,1)S(1)}, bf16[1152,448]{0,1:T(8,128)(2,1)}, u32[]{:S(2)}) copy-start(bf16[1152,448]{0,1:T(8,128)(2,1)} %param.21) | copy-start | bytes 3096580
  239.8 179.3 %reduce-scatter.4.cloned.1.call-start = ((), (), s32[]{:S(2)}) async-start(), calls=%async_computation.5 | async-start | bytes 1114112 | tf_op jit(solution)/shard_map/reduce_scatter | solution.py:88
Sparse Core Ops, SparseCore 0:
  36.7 45.0 all-gather.1
  85.0 111.1 all-reduce.2
  239.9 117.6 all-reduce.4
  362.0 57.0 reduce-scatter.3
where the time goes:
time: 428 us; the launch traced here: 427 us
  waiting for transfers between devices  328 us (77%)
  blocking collectives  55.9 us (13%)
  matrix products  18.3 us (4%)
  between operations  13.9 us (3%)
  other arithmetic  6.27 us (1%)
    psum x1, waiting for transfers between devices, local(): lax.psum(jnp.dot(normed, joined, preferred_element_type=jnp.float32), 'grp')  118 us
    psum x1, waiting for transfers between devices, local(): projected = lax.psum(partial_value, 'tp')  108 us
    reduce_scatter x1, waiting for transfers between devices, local(): lax.psum_scatter(terms, 'tp', scatter_dimension=0, tiled=True)  57.2 us
    all_gather x1, waiting for transfers between devices, local(): lax.all_gather(values, 'grp', axis=0, tiled=True)  45.2 us
    psum x1, blocking collectives, local(): squares = lax.psum(jnp.sum(combined_all * combined_all, axis=1), 'grp')  36.4 us
    all_to_all x1, blocking collectives, local(): lax.all_to_all(attended, 'tp', split_axis=1, concat_axis=0, tiled=True)  19.5 us
  transfers between devices with their start and end apart: 4, of which 4 were waited for; matrix products, arithmetic and copies ran while one was open for 1% of the time, Pallas kernels for 0%

commit v1 on v0

v1 whole, which is shorter than its diff:
```python
import jax
import jax.numpy as jnp
from jax import lax
from jax.sharding import Mesh, PartitionSpec as P

D = 7168
KL = 512
QKD = 192
GRP = ("y", "x")
TP = ("z", "c")
BF = jnp.bfloat16
F32 = jnp.float32


def exchange(parts, axes):
    return lax.all_to_all(parts, axes, split_axis=0, concat_axis=0, tiled=False)


def gather(block, axes, n):
    return exchange(jnp.broadcast_to(block[None], (n,) + block.shape), axes)


def attend(queries, cache, lengths):
    scores = jnp.einsum("rhk,rlk->rhl", queries, cache, preferred_element_type=F32)
    scores = scores * QKD ** (-0.5)
    place = lax.broadcasted_iota(jnp.int32, (1, 1, cache.shape[1]), 2)
    scores = jnp.where(place < lengths[:, None, None], scores, -jnp.inf)
    expo = jnp.exp(scores - jnp.max(scores, axis=2, keepdims=True))
    totals = jnp.sum(expo, axis=2, keepdims=True)
    summed = jnp.einsum(
        "rhl,rlk->rhk", expo.astype(BF), cache[:, :, :KL], preferred_element_type=F32
    )
    return summed / totals


def split_sum(x):
    high = x.astype(BF)
    return high, (x - high.astype(F32)).astype(BF)


def local(
    queries,
    latent_cache,
    lengths,
    counts,
    residual,
    value_up,
    out_proj,
    norm_gain,
    gate_up,
    down_proj,
):
    slots = queries.shape[0]
    heads = value_up.shape[0]
    n = 16
    in_use = lax.broadcasted_iota(jnp.int32, (slots,), 0) < counts[0]
    attended = jnp.where(
        in_use[:, None, None], attend(queries, latent_cache, lengths), 0.0
    ).astype(BF)
    received = lax.all_to_all(attended, TP, split_axis=1, concat_axis=0, tiled=True)
    values = jnp.einsum(
        "rhk,hkd->rhd", received, value_up, preferred_element_type=F32
    ).astype(BF)
    rows = values.shape[0]
    values = gather(values.reshape(rows, -1), GRP, n).reshape(n * rows, -1)
    partial = jnp.dot(values, out_proj, preferred_element_type=F32).astype(BF)
    share = partial.shape[0] // n
    pieces = exchange(partial.reshape(n, share, -1), TP)
    projected = jnp.sum(pieces.astype(F32), axis=0)
    offset = lax.axis_index(TP) * share
    mine = lax.dynamic_slice_in_dim(residual, offset, share, 0)
    combined = mine.astype(F32) + projected
    high, low = split_sum(jnp.sum(combined * combined, axis=1, keepdims=True))
    scaled = (combined * norm_gain.astype(F32)).astype(BF)
    feats = scaled.shape[1]
    packed = jnp.concatenate(
        [scaled, high, low, jnp.zeros((share, 512 - feats - 2), BF)], axis=1
    )
    packed = gather(packed, TP, n).reshape(n * share, 512)
    units = gate_up.shape[2]
    joined = gate_up.reshape(feats, 2 * units)
    terms = jnp.dot(packed[:, :feats], joined, preferred_element_type=F32).astype(BF)
    terms = jnp.concatenate([terms, packed[:, feats : feats + 2], jnp.zeros((n * share, 126), BF)], axis=1)
    summed = jnp.sum(
        exchange(terms.reshape(n, share, -1), GRP).astype(F32), axis=0
    )
    squares = summed[:, 2 * units] + summed[:, 2 * units + 1]
    factor = lax.rsqrt(squares / D + 1e-06)[:, None]
    gate = summed[:, :units] * factor
    up = summed[:, units : 2 * units] * factor
    hidden = (jax.nn.silu(gate) * up).astype(BF)
    hidden = gather(hidden, GRP, n).reshape(n * share, units)
    last = jnp.dot(hidden, down_proj, preferred_element_type=F32).astype(BF)
    last = exchange(last.reshape(n, share, -1), TP)
    return (combined + jnp.sum(last.astype(F32), axis=0)).astype(BF)


def solution(mesh):
    inner = Mesh(mesh.devices.reshape(4, 4, 8, 2), GRP + TP)
    every = GRP + TP
    placed = (
        P(every, None, None),
        P(every, None, None),
        P(every),
        P(every),
        P(None, GRP),
        P(TP, None, None),
        P(TP, GRP),
        P(GRP),
        P(GRP, None, TP),
        P(TP, GRP),
    )
    return jax.shard_map(
        local, mesh=inner, in_specs=placed, out_specs=P(TP, GRP), check_vma=False
    )
```

time: 428 us -> 187 us (0.44)
  the two profiles are of different devices: /device:TPU:2 before, /device:TPU:1 now
where the time goes in v1:
time: 187 us
  blocking collectives  123 us (66%)
  waiting for transfers between devices  30.4 us (16%)
  local copies, waits for them, and re-layouts  12.7 us (7%)
  starting transfers between devices  8.21 us (4%)
  matrix products  7.94 us (4%)
  other arithmetic  3.28 us (2%)
    all_to_all x4, blocking collectives, exchange(): return lax.all_to_all(parts, axes, split_axis=0, concat_axis=0, tiled=False)  102 us
    all_to_all x2, waiting for transfers between devices, exchange(): return lax.all_to_all(parts, axes, split_axis=0, concat_axis=0, tiled=False)  30.4 us
    all_to_all x1, blocking collectives, local(): lax.all_to_all(attended, TP, split_axis=1, concat_axis=0, tiled=True)  21.5 us
    all_to_all x2, starting transfers between devices, exchange(): return lax.all_to_all(parts, axes, split_axis=0, concat_axis=0, tiled=False)  8.21 us
    dot_general x1, matrix products, local(): jnp.dot(packed[:, :feats], joined, preferred_element_type=F32).astype(BF)  3.84 us
  transfers between devices with their start and end apart: 2, of which 2 were waited for; matrix products, arithmetic and copies ran while one was open for 2% of the time, Pallas kernels for 0%

profile of v1, /device:TPU:1, one launch (start us, length us, event | category | flops | bytes accessed | tf_op | source)
XLA Modules:
  0.0 186.6 jit_solution(8734979010091623571)
XLA Ops:
  0.0 0.0 copy-start
  0.0 0.0 copy-start.1
  0.0 0.9 iota_compare_fusion
  1.5 1.9 %fusion.19 = (f32[2,128]{1,0:T(2,128)S(1)}, f32[2,128,512]{2,1,0:T(8,128)S(1)}) fusion(bf16[2,128,576]{1,2,0:T(8,128)(2,1)} %param.10, bf16[2,512,576]{1,2,0:T(8,128)(2,1)} %param.11, pred[2,512]{1,0:T(4,128)(4,1)S(1)} %iota_compare_fusion), kind=kOutput, calls=%fused_computation.43 | convolution fusion | flops 151387904 | bytes 2000896 | tf_op jit(solution)/shard_map/rhk,rlk->rhl/dot_general | solution.py:24
  3.4 0.7 fusion
  4.1 0.0 copy-done.1
  4.1 0.5 fusion.3
  4.6 0.3 copy.37
  4.9 21.5 %all_to_all.48 = bf16[2,128,512]{2,0,1:T(2,128)(2,1)S(1)} all-to-all(bf16[2,128,512]{2,0,1:T(2,128)(2,1)S(1)} %copy.37), channel_id=1, replica_groups=mesh['y'=4,'x'=4,'z'=8,'c'=2] {'z','c'}, dimensions={1} | all-to-all | bytes 524288 | tf_op jit(solution)/shard_map/all_to_all | solution.py:60
  26.4 0.2 copy.50
  26.6 0.1 all_to_all.34
  26.7 0.0 copy-done
  26.7 0.0 copy-start.8
  26.7 0.3 fusion.4
  27.0 0.1 broadcast_in_dim.61
  27.1 24.0 %all_to_all.49 = bf16[16,32,1024]{2,1,0:T(8,128)(2,1)S(1)} all-to-all(bf16[16,32,1024]{2,1,0:T(8,128)(2,1)S(1)} %broadcast_in_dim.61), channel_id=1, replica_groups=mesh['y'=4,'x'=4,'z'=8,'c'=2] {'y','x'}, dimensions={0} | all-to-all | bytes 2097152 | tf_op jit(solution)/shard_map/all_to_all | solution.py:16
  51.1 0.0 copy-done.8
  51.1 0.0 copy-start.6
  51.1 0.7 convolution_convert_fusion.2
  51.8 1.0 copy.40
  52.8 4.1 %all-to-all-start.2 = ((bf16[16,32,448]{2,1,0:T(8,128)(2,1)}), bf16[16,32,448]{2,1,0:T(8,128)(2,1)S(1)}, u32[]{:S(2)}, u32[]{:S(2)}) async-start(bf16[16,32,448]{2,1,0:T(8,128)(2,1)} %bitcast.5), calls=%async_computation.2 | async-start | bytes 1048576 | tf_op jit(solution)/shard_map/all_to_all | solution.py:16
  56.9 1.0 constant_dynamic-slice_fusion
  57.9 0.1 copy.44
  58.0 0.0 copy-done.6
  58.0 0.0 copy-start.4
  58.0 0.1 pad.3.clone
  58.1 16.1 %all-to-all-done.2 = bf16[16,32,448]{2,1,0:T(8,128)(2,1)S(1)} async-done(((bf16[16,32,448]{2,1,0:T(8,128)(2,1)}), bf16[16,32,448]{2,1,0:T(8,128)(2,1)S(1)}, u32[]{:S(2)}, u32[]{:S(2)}) %all-to-all-start.2) | async-done | bytes 458784 | tf_op jit(solution)/shard_map/all_to_all | solution.py:16
  74.2 0.1 convert_reduce_fusion.2
  74.3 0.0 copy-start.2
  74.3 0.6 copy-done.2
  74.9 0.1 multiply_convert_fusion
  75.1 0.1 copy.41
  75.2 0.1 copy.42
  75.3 0.1 maximum_maximum_fusion
  75.4 0.8 broadcast_in_dim.63
  76.2 4.1 %all-to-all-start.3 = ((bf16[16,32,512]{2,1,0:T(8,128)(2,1)}), bf16[16,32,512]{2,1,0:T(8,128)(2,1)}, u32[]{:S(2)}, u32[]{:S(2)}) async-start(bf16[16,32,512]{2,1,0:T(8,128)(2,1)} %broadcast_in_dim.63), calls=%async_computation.3 | async-start | bytes 1048576 | tf_op jit(solution)/shard_map/all_to_all | solution.py:16
  80.4 0.0 copy-done.4
  80.4 1.9 %copy.47 = bf16[56,8,2,1152]{3,1,2,0:T(8,128)(2,1)S(1)} copy(bf16[56,8,2,1152]{3,2,1,0:T(2,128)(2,1)} %bitcast.40) | data formatting | bytes 4128768
  82.3 14.3 %all-to-all-done.3 = bf16[16,32,512]{2,1,0:T(8,128)(2,1)} async-done(((bf16[16,32,512]{2,1,0:T(8,128)(2,1)}), bf16[16,32,512]{2,1,0:T(8,128)(2,1)}, u32[]{:S(2)}, u32[]{:S(2)}) %all-to-all-start.3) | async-done | bytes 524320 | tf_op jit(solution)/shard_map/all_to_all | solution.py:16
  96.6 1.7 slice.29
  98.2 3.8 %convolution_convert_fusion = bf16[512,2304]{1,0:T(8,128)(2,1)} fusion(bf16[448,2304]{1,0:T(8,128)(2,1)S(1)} %bitcast.41, bf16[512,512]{1,0:T(8,128)(2,1)} %bitcast.7), kind=kOutput, calls=%fused_computation.2 | convolution fusion | flops 1058144256 | bytes 4947968 | tf_op jit(solution)/shard_map/dot_general | solution.py:82
  102.1 0.7 broadcast_in_dim.64
  102.7 3.6 %concatenate.7 = bf16[512,2432]{1,0:T(8,128)(2,1)S(1)} concatenate(bf16[512,2304]{1,0:T(8,128)(2,1)} %convolution_convert_fusion, bf16[512,2]{1,0:T(8,128)(2,1)} %slice.29, bf16[512,126]{1,0:T(8,128)(2,1)} %broadcast_in_dim.64), dimensions={1} | concatenate | bytes 4980736 | tf_op jit(solution)/shard_map/concatenate | solution.py:83
  106.4 35.6 %all_to_all.50 = bf16[16,32,2432]{2,1,0:T(8,128)(2,1)S(1)} all-to-all(bf16[16,32,2432]{2,1,0:T(8,128)(2,1)S(1)} %bitcast.38), channel_id=1, replica_groups=mesh['y'=4,'x'=4,'z'=8,'c'=2] {'y','x'}, dimensions={0} | all-to-all | bytes 4980736 | tf_op jit(solution)/shard_map/all_to_all | solution.py:16
  141.9 0.4 convert_reduce_fusion
  142.3 0.0 copy-start.7
  142.3 0.2 fusion.17
  142.5 0.1 fusion.13
  142.6 0.1 broadcast_in_dim.65
  142.7 20.3 %all_to_all.51 = bf16[16,32,1152]{2,1,0:T(8,128)(2,1)S(1)} all-to-all(bf16[16,32,1152]{2,1,0:T(8,128)(2,1)S(1)} %broadcast_in_dim.65), channel_id=1, replica_groups=mesh['y'=4,'x'=4,'z'=8,'c'=2] {'y','x'}, dimensions={0} | all-to-all | bytes 2359296 | tf_op jit(solution)/shard_map/all_to_all | solution.py:16
  163.0 0.0 copy-done.7
  163.0 0.8 convolution_convert_fusion.1
  163.8 0.0 copy-start.3
  163.8 0.0 copy-start.5
  163.8 0.2 copy.43
  164.0 21.8 %all_to_all.52 = bf16[16,32,448]{2,1,0:T(8,128)(2,1)S(1)} all-to-all(bf16[16,32,448]{2,1,0:T(8,128)(2,1)S(1)} %bitcast.39), channel_id=1, replica_groups=mesh['y'=4,'x'=4,'z'=8,'c'=2] {'z','c'}, dimensions={0} | all-to-all | bytes 917504 | tf_op jit(solution)/shard_map/all_to_all | solution.py:16
  185.8 0.1 convert_reduce_fusion.1
  185.9 0.0 copy-done.3
  185.9 0.0 copy-done.5
  185.9 0.6 add_convert_fusion
  (6 shorter events, 0.0 us)
Async XLA Ops:
  0.0 26.7 %copy-start = (bf16[8,512,128]{2,1,0:T(8,128)(2,1)S(1)}, bf16[8,512,128]{2,1,0:T(8,128)(2,1)}, u32[]{:S(2)}) copy-start(bf16[8,512,128]{2,1,0:T(8,128)(2,1)} %param.15) | copy-start | bytes 3145732
  0.0 4.1 %copy-start.1 = (bf16[2,512,576]{1,2,0:T(8,128)(2,1)S(1)}, bf16[2,512,576]{1,2,0:T(8,128)(2,1)}, u32[]{:S(2)}) copy-start(bf16[2,512,576]{1,2,0:T(8,128)(2,1)} %param.11) | copy-start | bytes 3538948
  26.7 24.4 %copy-start.8 = (bf16[1024,448]{0,1:T(8,128)(2,1)S(1)}, bf16[1024,448]{0,1:T(8,128)(2,1)}, u32[]{:S(2)}) copy-start(bf16[1024,448]{0,1:T(8,128)(2,1)} %param.16) | copy-start | bytes 2752516
  51.1 6.8 %copy-start.6 = (bf16[448]{0:T(512)(128)(2,1)S(1)}, bf16[448]{0:T(512)(128)(2,1)}, u32[]{:S(2)}) copy-start(bf16[448]{0:T(512)(128)(2,1)} %param.17) | copy-start | bytes 2692
  52.8 21.4 %all-to-all-start.2 = ((bf16[16,32,448]{2,1,0:T(8,128)(2,1)}), bf16[16,32,448]{2,1,0:T(8,128)(2,1)S(1)}, u32[]{:S(2)}, u32[]{:S(2)}) async-start(bf16[16,32,448]{2,1,0:T(8,128)(2,1)} %bitcast.5), calls=%async_computation.2 | async-start | bytes 1048576 | tf_op jit(solution)/shard_map/all_to_all | solution.py:16
  58.0 22.4 %copy-start.4 = (bf16[32,448]{1,0:T(8,128)(2,1)}, bf16[32,448]{1,0:T(8,128)(2,1)S(1)}, u32[]{:S(2)}) copy-start(bf16[32,448]{1,0:T(8,128)(2,1)S(1)} %copy.44) | copy-start | bytes 86020
  74.3 0.6 copy-start.2
  76.2 20.3 %all-to-all-start.3 = ((bf16[16,32,512]{2,1,0:T(8,128)(2,1)}), bf16[16,32,512]{2,1,0:T(8,128)(2,1)}, u32[]{:S(2)}, u32[]{:S(2)}) async-start(bf16[16,32,512]{2,1,0:T(8,128)(2,1)} %broadcast_in_dim.63), calls=%async_computation.3 | async-start | bytes 1048576 | tf_op jit(solution)/shard_map/all_to_all | solution.py:16
  142.3 20.7 %copy-start.7 = (bf16[1152,448]{0,1:T(8,128)(2,1)S(1)}, bf16[1152,448]{0,1:T(8,128)(2,1)}, u32[]{:S(2)}) copy-start(bf16[1152,448]{0,1:T(8,128)(2,1)} %param.19) | copy-start | bytes 3096580
  163.8 22.1 %copy-start.3 = (f32[32,448]{1,0:T(8,128)S(1)}, f32[32,448]{1,0:T(8,128)}, u32[]{:S(2)}) copy-start(f32[32,448]{1,0:T(8,128)} %copy-done.2) | copy-start | bytes 172036
  163.8 22.1 %copy-start.5 = (bf16[32,448]{1,0:T(8,128)(2,1)S(1)}, bf16[32,448]{1,0:T(8,128)(2,1)}, u32[]{:S(2)}) copy-start(bf16[32,448]{1,0:T(8,128)(2,1)} %copy-done.4) | copy-start | bytes 86020

commit v2 on v1

v2 whole, which is shorter than its diff:
```python
import jax
import jax.numpy as jnp
from jax import lax
from jax.sharding import Mesh, PartitionSpec as P

D = 7168
KL = 512
QKD = 192
GRP = ("y", "x")
TP = ("z", "c")
BF = jnp.bfloat16
F32 = jnp.float32


def exchange(parts, axes):
    return lax.all_to_all(parts, axes, split_axis=0, concat_axis=0, tiled=False)


def gather(block, axes, n):
    return exchange(jnp.broadcast_to(block[None], (n,) + block.shape), axes)


def attend(queries, cache, lengths):
    scores = jnp.einsum("rhk,rlk->rhl", queries, cache, preferred_element_type=F32)
    scores = scores * QKD ** (-0.5)
    place = lax.broadcasted_iota(jnp.int32, (1, 1, cache.shape[1]), 2)
    scores = jnp.where(place < lengths[:, None, None], scores, -jnp.inf)
    expo = jnp.exp(scores - jnp.max(scores, axis=2, keepdims=True))
    totals = jnp.sum(expo, axis=2, keepdims=True)
    summed = jnp.einsum(
        "rhl,rlk->rhk", expo.astype(BF), cache[:, :, :KL], preferred_element_type=F32
    )
    return summed / totals


def split_sum(x):
    high = x.astype(BF)
    return high, (x - high.astype(F32)).astype(BF)


def local(
    queries,
    latent_cache,
    lengths,
    counts,
    residual,
    value_up,
    out_proj,
    norm_gain,
    gate_up,
    down_proj,
):
    slots = queries.shape[0]
    core = lax.axis_index("c")
    value_up, out_proj, gate_up, down_proj = [
        (w, lax.ppermute(w, "c", [(0, 1), (1, 0)]))
        for w in (value_up, out_proj, gate_up, down_proj)
    ]
    in_use = lax.broadcasted_iota(jnp.int32, (slots,), 0) < counts[0]
    attended = jnp.where(
        in_use[:, None, None], attend(queries, latent_cache, lengths), 0.0
    ).astype(BF)
    paired = attended.reshape(slots, 8, 2, 8, KL)
    paired = jnp.where(core == 0, paired, paired[:, :, ::-1])
    paired = jnp.transpose(paired, (1, 0, 2, 3, 4))
    received = exchange(paired, "z").reshape(8 * slots, 2, 8, KL)
    values = [
        jnp.einsum(
            "rhk,hkd->rhd", received[:, i], value_up[i], preferred_element_type=F32
        )
        .astype(BF)
        .reshape(8 * slots, -1)
        for i in range(2)
    ]
    values = gather(jnp.concatenate(values, axis=1), GRP, 16).reshape(256, -1)
    depth = out_proj[0].shape[0]
    partial = sum(
        jnp.dot(
            values[:, i * depth : (i + 1) * depth],
            out_proj[i],
            preferred_element_type=F32,
        )
        for i in range(2)
    ).astype(BF)
    feats = partial.shape[1]
    pieces = exchange(partial.reshape(16, 16, feats), TP)
    projected = jnp.sum(pieces.astype(F32).reshape(8, 2, 8, 2, feats), axis=0)
    projected = jnp.transpose(projected, (1, 0, 2, 3)).reshape(32, feats)
    offset = lax.axis_index(TP) * 32
    mine = lax.dynamic_slice_in_dim(residual, offset, 32, 0)
    combined = mine.astype(F32) + projected
    high, low = split_sum(jnp.sum(combined * combined, axis=1, keepdims=True))
    scaled = (combined * norm_gain.astype(F32)).astype(BF)
    packed = jnp.concatenate(
        [scaled, high, low, jnp.zeros((32, 512 - feats - 2), BF)], axis=1
    )
    packed = gather(packed, "z", 8).reshape(256, 512)
    units = gate_up[0].shape[2]
    terms = [
        jnp.dot(
            packed[:, :feats], w.reshape(feats, 2 * units), preferred_element_type=F32
        ).astype(BF)
        for w in gate_up
    ]
    terms = jnp.concatenate(
        terms + [packed[:, feats : feats + 2], jnp.zeros((256, 126), BF)], axis=1
    )
    summed = jnp.sum(exchange(terms.reshape(16, 16, -1), GRP).astype(F32), axis=0)
    squares = summed[:, 4 * units] + summed[:, 4 * units + 1]
    factor = lax.rsqrt(squares / D + 1e-06)[:, None]
    hidden = []
    for i in range(2):
        gate = summed[:, 2 * i * units : (2 * i + 1) * units] * factor
        up = summed[:, (2 * i + 1) * units : (2 * i + 2) * units] * factor
        hidden.append((jax.nn.silu(gate) * up).astype(BF))
    hidden = gather(jnp.concatenate(hidden, axis=1), GRP, 16).reshape(256, 2 * units)
    last = sum(
        jnp.dot(
            hidden[:, i * units : (i + 1) * units],
            down_proj[i],
            preferred_element_type=F32,
        )
        for i in range(2)
    ).astype(BF)
    last = exchange(last.reshape(8, 32, feats), "z")
    return (combined + jnp.sum(last.astype(F32), axis=0)).astype(BF)


def solution(mesh):
    inner = Mesh(mesh.devices.reshape(4, 4, 8, 2), GRP + TP)
    every = GRP + TP
    placed = (
        P(every, None, None),
        P(every, None, None),
        P(every),
        P(every),
        P(None, GRP),
        P(TP, None, None),
        P(TP, GRP),
        P(GRP),
        P(GRP, None, TP),
        P(TP, GRP),
    )
    return jax.shard_map(
        local, mesh=inner, in_specs=placed, out_specs=P(TP, GRP), check_vma=False
    )
```

time: 187 us -> 172 us (0.920)
  the two profiles are of different devices: /device:TPU:1 before, /device:TPU:2 now
where the time goes in v2:
time: 172 us; the launch traced here: 171 us
  blocking collectives  69.3 us (40%)
  waiting for transfers between devices  50.9 us (30%)
  starting transfers between devices  20 us (12%)
  local copies, waits for them, and re-layouts  13.8 us (8%)
  matrix products  12.4 us (7%)
  other arithmetic  3.39 us (2%)
    all_to_all x3, blocking collectives, exchange(): return lax.all_to_all(parts, axes, split_axis=0, concat_axis=0, tiled=False)  69.3 us
    all_to_all x4, waiting for transfers between devices, exchange(): return lax.all_to_all(parts, axes, split_axis=0, concat_axis=0, tiled=False)  50.9 us
    all_to_all x4, starting transfers between devices, exchange(): return lax.all_to_all(parts, axes, split_axis=0, concat_axis=0, tiled=False)  19.4 us
    dot_general x2, matrix products, local(): jnp.dot(packed[:, :feats], w.reshape(feats, 2 * units), preferred_element...  5.2 us
    unnamed x15, local copies, waits for them, and re-layouts  5.14 us
    concatenate x1, local copies, waits for them, and re-layouts, local(): jnp.concatenate(terms + [packed[:, feats:feats + 2], jnp.zeros((256, 126)...  3.78 us
  transfers between devices with their start and end apart: 8, of which 4 were waited for; matrix products, arithmetic and copies ran while one was open for 9% of the time, Pallas kernels for 0%

profile of v2, /device:TPU:2, one launch (start us, length us, event | category | flops | bytes accessed | tf_op | source)
XLA Modules:
  0.0 170.7 jit_solution(7257132413674103866)
XLA Ops:
  0.0 0.0 copy-start
  0.0 0.0 copy-start.1
  0.0 0.0 collective-permute-start
  0.0 0.8 iota_compare_fusion
  1.5 1.9 %fusion.33 = (f32[2,128]{1,0:T(2,128)S(1)}, f32[2,128,512]{2,1,0:T(8,128)S(1)}) fusion(bf16[2,128,576]{1,2,0:T(8,128)(2,1)} %param.10, bf16[2,512,576]{1,2,0:T(8,128)(2,1)} %param.11, pred[2,512]{1,0:T(4,128)(4,1)S(1)} %iota_compare_fusion), kind=kOutput, calls=%fused_computation.65 | convolution fusion | flops 151387904 | bytes 2000896 | tf_op jit(solution)/shard_map/rhk,rlk->rhl/dot_general | solution.py:24
  3.4 0.7 fusion
  4.1 0.0 copy-done.1
  4.1 0.5 fusion.3
  4.7 0.1 fusion.17
  4.7 20.7 %all_to_all.35 = bf16[8,2,2,8,512]{4,3,2,1,0:T(8,128)(2,1)S(1)} all-to-all(bf16[8,2,2,8,512]{4,3,2,1,0:T(8,128)(2,1)S(1)} %fusion.17), channel_id=1, replica_groups=mesh['y'=4,'x'=4,'z'=8,'c'=2] {'z'}, dimensions={0} | all-to-all | bytes 524288 | tf_op jit(solution)/shard_map/all_to_all | solution.py:16
  25.4 0.0 copy-done.2
  25.4 0.3 fusion.6
  25.7 0.0 collective-permute-done
  25.7 0.0 copy-start.4
  25.7 0.3 fusion.7
  26.0 1.1 broadcast_in_dim.59
  27.1 7.5 %all-to-all-start.1 = ((bf16[16,16,2048]{2,1,0:T(8,128)(2,1)}), bf16[16,16,2048]{2,1,0:T(8,128)(2,1)S(1)}, u32[]{:S(2)}, u32[]{:S(2)}) async-start(bf16[16,16,2048]{2,1,0:T(8,128)(2,1)} %broadcast_in_dim.59), calls=%async_computation.1 | async-start | bytes 2097152 | tf_op jit(solution)/shard_map/all_to_all | solution.py:16
  34.6 0.0 copy-done.4
  34.6 0.1 collective-permute-start.1
  34.7 0.5 collective-permute-start.2
  35.2 15.3 %all-to-all-done.1 = bf16[16,16,2048]{2,1,0:T(8,128)(2,1)S(1)} async-done(((bf16[16,16,2048]{2,1,0:T(8,128)(2,1)}), bf16[16,16,2048]{2,1,0:T(8,128)(2,1)S(1)}, u32[]{:S(2)}, u32[]{:S(2)}) %all-to-all-start.1) | async-done | bytes 1048608 | tf_op jit(solution)/shard_map/all_to_all | solution.py:16
  50.5 0.4 fusion.13
  51.0 0.0 copy-start.5
  51.0 0.0 collective-permute-done.1
  51.0 1.6 fusion.4
  52.6 0.9 copy.57
  53.5 3.5 %all-to-all-start.2 = ((bf16[16,16,448]{2,1,0:T(8,128)(2,1)}), bf16[16,16,448]{2,1,0:T(8,128)(2,1)S(1)}, u32[]{:S(2)}, u32[]{:S(2)}) async-start(bf16[16,16,448]{2,1,0:T(8,128)(2,1)} %bitcast.9), calls=%async_computation.2 | async-start | bytes 524288 | tf_op jit(solution)/shard_map/all_to_all | solution.py:16
  57.1 0.0 copy-done
  57.1 0.1 constant_dynamic-slice_fusion
  57.2 0.1 copy.63
  57.3 0.0 copy-done.5
  57.3 0.1 pad.5.clone
  57.4 10.7 %all-to-all-done.2 = bf16[16,16,448]{2,1,0:T(8,128)(2,1)S(1)} async-done(((bf16[16,16,448]{2,1,0:T(8,128)(2,1)}), bf16[16,16,448]{2,1,0:T(8,128)(2,1)S(1)}, u32[]{:S(2)}, u32[]{:S(2)}) %all-to-all-start.2) | async-done | bytes 229408 | tf_op jit(solution)/shard_map/all_to_all | solution.py:16
  68.0 0.3 reshape.116
  68.4 0.2 reduce_sum.48
  68.7 0.1 multiply_convert_fusion
  68.8 0.1 copy.59
  68.9 0.1 copy.60
  69.0 0.1 maximum_maximum_fusion
  69.1 0.7 broadcast_in_dim.61
  69.8 3.4 %all-to-all-start.3 = ((bf16[8,32,512]{2,1,0:T(8,128)(2,1)}), bf16[8,32,512]{2,1,0:T(8,128)(2,1)S(1)}, u32[]{:S(2)}, u32[]{:S(2)}) async-start(bf16[8,32,512]{2,1,0:T(8,128)(2,1)} %broadcast_in_dim.61), calls=%async_computation.3 | async-start | bytes 524288 | tf_op jit(solution)/shard_map/all_to_all | solution.py:16
  73.2 1.9 %copy.69 = bf16[56,8,2,1152]{3,1,2,0:T(8,128)(2,1)S(1)} copy(bf16[56,8,2,1152]{3,2,1,0:T(2,128)(2,1)} %bitcast.62) | data formatting | bytes 4128768
  75.1 0.0 collective-permute-done.2
  75.1 3.2 %copy.70 = bf16[56,8,2,1152]{3,1,2,0:T(8,128)(2,1)} copy(bf16[56,8,2,1152]{3,2,1,0:T(2,128)(2,1)} %bitcast.22) | data formatting | bytes 4128768
  78.3 8.2 %all-to-all-done.3 = bf16[8,32,512]{2,1,0:T(8,128)(2,1)S(1)} async-done(((bf16[8,32,512]{2,1,0:T(8,128)(2,1)}), bf16[8,32,512]{2,1,0:T(8,128)(2,1)S(1)}, u32[]{:S(2)}, u32[]{:S(2)}) %all-to-all-start.3) | async-done | bytes 262176 | tf_op jit(solution)/shard_map/all_to_all | solution.py:16
  86.5 0.1 slice.66
  86.6 3.4 %convolution_convert_fusion = bf16[256,2304]{1,0:T(8,128)(2,1)} fusion(bf16[448,2304]{1,0:T(8,128)(2,1)} %bitcast.54, bf16[256,512]{1,0:T(8,128)(2,1)S(1)} %bitcast.60), kind=kOutput, calls=%fused_computation.2 | convolution fusion | flops 529072128 | bytes 3506176 | tf_op jit(solution)/shard_map/dot_general | solution.py:100
  90.0 1.8 %convolution_convert_fusion.1 = bf16[256,2304]{1,0:T(8,128)(2,1)} fusion(bf16[448,2304]{1,0:T(8,128)(2,1)S(1)} %bitcast.53, bf16[256,512]{1,0:T(8,128)(2,1)S(1)} %bitcast.61), kind=kOutput, calls=%fused_computation.3 | convolution fusion | flops 529072128 | bytes 3506176 | tf_op jit(solution)/shard_map/dot_general | solution.py:100
  91.8 3.8 %concatenate.14 = bf16[256,4736]{1,0:T(8,128)(2,1)S(1)} concatenate(bf16[256,2304]{1,0:T(8,128)(2,1)} %convolution_convert_fusion.1, bf16[256,2304]{1,0:T(8,128)(2,1)} %convolution_convert_fusion, bf16[256,2]{1,0:T(8,128)(2,1)S(1)} %slice.66, bf16[256,126]{1,0:T(8,128)(2,1)S(1)} %broadcast_in_dim.62), dimensions={1} | concatenate | bytes 4849664 | tf_op jit(solution)/shard_map/concatenate | solution.py:105
  95.6 35.7 %all_to_all.36 = bf16[16,16,4736]{2,1,0:T(8,128)(2,1)S(1)} all-to-all(bf16[16,16,4736]{2,1,0:T(8,128)(2,1)S(1)} %bitcast.52), channel_id=1, replica_groups=mesh['y'=4,'x'=4,'z'=8,'c'=2] {'y','x'}, dimensions={0} | all-to-all | bytes 4849664 | tf_op jit(solution)/shard_map/all_to_all | solution.py:16
  131.3 0.3 convert_reduce_fusion
  131.7 0.2 fusion.30
  131.8 0.1 fusion.26
  132.0 1.1 broadcast_in_dim.63
  133.1 4.9 %all-to-all-start.5 = ((bf16[16,16,2304]{2,1,0:T(8,128)(2,1)}), bf16[16,16,2304]{2,1,0:T(8,128)(2,1)S(1)}, u32[]{:S(2)}, u32[]{:S(2)}) async-start(bf16[16,16,2304]{2,1,0:T(8,128)(2,1)} %broadcast_in_dim.63), calls=%async_computation.5 | async-start | bytes 2359296 | tf_op jit(solution)/shard_map/all_to_all | solution.py:16
  138.0 0.0 copy-done.3
  138.0 0.1 collective-permute-start.3
  138.1 16.7 %all-to-all-done.5 = bf16[16,16,2304]{2,1,0:T(8,128)(2,1)S(1)} async-done(((bf16[16,16,2304]{2,1,0:T(8,128)(2,1)}), bf16[16,16,2304]{2,1,0:T(8,128)(2,1)S(1)}, u32[]{:S(2)}, u32[]{:S(2)}) %all-to-all-start.5) | async-done | bytes 1179680 | tf_op jit(solution)/shard_map/all_to_all | solution.py:16
  154.8 0.5 fusion.10
  155.3 0.0 collective-permute-done.3
  155.3 1.7 %fusion.5 = bf16[256,448]{0,1:T(8,128)(2,1)S(1)} fusion(f32[256,448]{0,1:T(8,128)S(1)} %fusion.10, bf16[1152,448]{0,1:T(8,128)(2,1)} %collective-permute-done.3, bf16[256,2304]{1,0:T(8,128)(2,1)S(1)} %bitcast.56), kind=kOutput, calls=%fused_computation.12 | convolution fusion | flops 264470528 | bytes 2310144 | tf_op jit(solution)/shard_map/dot_general | solution.py:118
  157.0 0.1 copy.61
  157.2 12.9 %all_to_all.37 = bf16[8,32,448]{2,1,0:T(8,128)(2,1)S(1)} all-to-all(bf16[8,32,448]{2,1,0:T(8,128)(2,1)S(1)} %bitcast.64), channel_id=1, replica_groups=mesh['y'=4,'x'=4,'z'=8,'c'=2] {'z'}, dimensions={0} | all-to-all | bytes 458752 | tf_op jit(solution)/shard_map/all_to_all | solution.py:16
  170.1 0.6 add_convert_fusion
  (17 shorter events, 0.2 us)
Async XLA Ops:
  0.0 57.1 %copy-start = (bf16[512,448]{0,1:T(8,128)(2,1)S(1)}, bf16[512,448]{0,1:T(8,128)(2,1)}, u32[]{:S(2)}) copy-start(bf16[512,448]{0,1:T(8,128)(2,1)} %param.14) | copy-start | bytes 1376260
  0.0 4.1 %copy-start.1 = (bf16[2,512,576]{1,2,0:T(8,128)(2,1)S(1)}, bf16[2,512,576]{1,2,0:T(8,128)(2,1)}, u32[]{:S(2)}) copy-start(bf16[2,512,576]{1,2,0:T(8,128)(2,1)} %param.11) | copy-start | bytes 3538948
  0.0 25.7 %collective-permute-start = (bf16[8,512,128]{2,1,0:T(8,128)(2,1)}, bf16[8,512,128]{2,1,0:T(8,128)(2,1)S(1)}, u32[]{:S(2)}, u32[]{:S(2)}) collective-permute-start(bf16[8,512,128]{2,1,0:T(8,128)(2,1)} %param.15), channel_id=1, source_target_pairs={{0,1},{1,0},{2,3},{3,2},{4,5},{5,4},{6,7},{7,6},{8,9},{9,8},{10,11... | collective-permute-start | bytes 3145736 | tf_op jit(solution)/shard_map/ppermute | solution.py:56
  4.1 21.3 %copy-start.2 = (bf16[8,512,128]{2,1,0:T(8,128)(2,1)S(1)}, bf16[8,512,128]{2,1,0:T(8,128)(2,1)}, u32[]{:S(2)}) copy-start(bf16[8,512,128]{2,1,0:T(8,128)(2,1)} %param.15) | copy-start | bytes 3145732
  25.7 8.9 %copy-start.4 = (bf16[1024,448]{0,1:T(8,128)(2,1)S(1)}, bf16[1024,448]{0,1:T(8,128)(2,1)}, u32[]{:S(2)}) copy-start(bf16[1024,448]{0,1:T(8,128)(2,1)} %param.16) | copy-start | bytes 2752516
  27.1 23.4 %all-to-all-start.1 = ((bf16[16,16,2048]{2,1,0:T(8,128)(2,1)}), bf16[16,16,2048]{2,1,0:T(8,128)(2,1)S(1)}, u32[]{:S(2)}, u32[]{:S(2)}) async-start(bf16[16,16,2048]{2,1,0:T(8,128)(2,1)} %broadcast_in_dim.59), calls=%async_computation.1 | async-start | bytes 2097152 | tf_op jit(solution)/shard_map/all_to_all | solution.py:16
  34.6 16.4 %collective-permute-start.1 = (bf16[1024,448]{0,1:T(8,128)(2,1)S(1)}, bf16[1024,448]{0,1:T(8,128)(2,1)}, u32[]{:S(2)}, u32[]{:S(2)}) collective-permute-start(bf16[1024,448]{0,1:T(8,128)(2,1)S(1)} %copy-done.4), channel_id=1, source_target_pairs={{0,1},{1,0},{2,3},{3,2},{4,5},{5,4},{6,7},{7,6},{8,9},{9,8},{10,11... | collective-permute-start | bytes 2752520 | tf_op jit(solution)/shard_map/ppermute | solution.py:56
  34.7 40.4 %collective-permute-start.2 = (bf16[448,2,1152]{2,1,0:T(2,128)(2,1)}, bf16[448,2,1152]{2,1,0:T(2,128)(2,1)}, u32[]{:S(2)}, u32[]{:S(2)}) collective-permute-start(bf16[448,2,1152]{2,1,0:T(2,128)(2,1)} %param.18), channel_id=1, source_target_pairs={{0,1},{1,0},{2,3},{3,2},{4,5},{5,4},{6,7},{7,6},{8,9},{9,8},{10,11... | collective-permute-start | bytes 6193160 | tf_op jit(solution)/shard_map/ppermute | solution.py:56
  51.0 6.3 %copy-start.5 = (bf16[448]{0:T(512)(128)(2,1)S(1)}, bf16[448]{0:T(512)(128)(2,1)}, u32[]{:S(2)}) copy-start(bf16[448]{0:T(512)(128)(2,1)} %param.17) | copy-start | bytes 2692
  53.5 14.5 %all-to-all-start.2 = ((bf16[16,16,448]{2,1,0:T(8,128)(2,1)}), bf16[16,16,448]{2,1,0:T(8,128)(2,1)S(1)}, u32[]{:S(2)}, u32[]{:S(2)}) async-start(bf16[16,16,448]{2,1,0:T(8,128)(2,1)} %bitcast.9), calls=%async_computation.2 | async-start | bytes 524288 | tf_op jit(solution)/shard_map/all_to_all | solution.py:16
  69.8 16.7 %all-to-all-start.3 = ((bf16[8,32,512]{2,1,0:T(8,128)(2,1)}), bf16[8,32,512]{2,1,0:T(8,128)(2,1)S(1)}, u32[]{:S(2)}, u32[]{:S(2)}) async-start(bf16[8,32,512]{2,1,0:T(8,128)(2,1)} %broadcast_in_dim.61), calls=%async_computation.3 | async-start | bytes 524288 | tf_op jit(solution)/shard_map/all_to_all | solution.py:16
  131.8 6.2 %copy-start.3 = (bf16[1152,448]{0,1:T(8,128)(2,1)S(1)}, bf16[1152,448]{0,1:T(8,128)(2,1)}, u32[]{:S(2)}) copy-start(bf16[1152,448]{0,1:T(8,128)(2,1)} %param.19) | copy-start | bytes 3096580
  133.1 21.7 %all-to-all-start.5 = ((bf16[16,16,2304]{2,1,0:T(8,128)(2,1)}), bf16[16,16,2304]{2,1,0:T(8,128)(2,1)S(1)}, u32[]{:S(2)}, u32[]{:S(2)}) async-start(bf16[16,16,2304]{2,1,0:T(8,128)(2,1)} %broadcast_in_dim.63), calls=%async_computation.5 | async-start | bytes 2359296 | tf_op jit(solution)/shard_map/all_to_all | solution.py:16
  138.0 17.3 %collective-permute-start.3 = (bf16[1152,448]{0,1:T(8,128)(2,1)S(1)}, bf16[1152,448]{0,1:T(8,128)(2,1)}, u32[]{:S(2)}, u32[]{:S(2)}) collective-permute-start(bf16[1152,448]{0,1:T(8,128)(2,1)S(1)} %copy-done.3), channel_id=1, source_target_pairs={{0,1},{1,0},{2,3},{3,2},{4,5},{5,4},{6,7},{7,6},{8,9},{9,8},{10,11... | collective-permute-start | bytes 3096584 | tf_op jit(solution)/shard_map/ppermute | solution.py:56

commit v3 on v1

v3 whole, which is shorter than its diff:
```python
import jax
import jax.numpy as jnp
from jax import lax
from jax.experimental import pallas as pl
from jax.experimental.pallas import tpu as pltpu
from jax.sharding import Mesh, PartitionSpec as P

D = 7168
KL = 512
QKD = 192
GRP = ("y", "x")
TP = ("z", "c")
BF = jnp.bfloat16
F32 = jnp.float32


def exchange(parts, axes):
    return lax.all_to_all(parts, axes, split_axis=0, concat_axis=0, tiled=False)


def call(body, shapes, *args, smem=0, limit=40):
    return pl.pallas_call(
        body,
        out_shape=shapes,
        in_specs=[
            pl.BlockSpec(memory_space=pltpu.SMEM if i < smem else pltpu.VMEM)
            for i in range(len(args))
        ],
        compiler_params=pltpu.CompilerParams(vmem_limit_bytes=limit * 2**20),
    )(*args)


def iota(shape, dim):
    return lax.broadcasted_iota(jnp.int32, shape, dim)


def mm(a, b):
    return jnp.dot(a, b, preferred_element_type=F32)


def mm_t(a, b):
    return lax.dot_general(a, b, (((1,), (1,)), ((), ())), preferred_element_type=F32)


def attend_body(lengths, counts, q_ref, c_ref, o_ref):
    for slot in range(2):
        query = q_ref[slot].T
        scores = mm(query, c_ref[slot]) * QKD ** (-0.5)
        scores = jnp.where(iota(scores.shape, 1) < lengths[slot], scores, -jnp.inf)
        expo = jnp.exp(scores - jnp.max(scores, axis=1, keepdims=True))
        scale = 1.0 / jnp.sum(expo, axis=1, keepdims=True)
        summed = mm_t(expo.astype(BF), c_ref[slot, :KL, :])
        summed = jnp.where(slot < counts[0], summed * scale, 0.0)
        o_ref[:, slot] = summed.astype(BF).reshape(8, 16, KL)


def value_body(core, x_ref, own_ref, other_ref, o_ref):
    x = x_ref[...]
    pick = ((iota((256, 256), 0) & 15) == (iota((256, 256), 1) >> 4)).astype(BF)
    head = (iota((256, 256), 0) & 15) - (iota((256, 256), 1) >> 7)
    for i, w_ref in enumerate((own_ref, other_ref)):
        first = 8 * (core[0] if i == 0 else 1 - core[0])
        for j in range(0, 8, 2):
            w = jnp.concatenate([w_ref[j], w_ref[j + 1]], axis=1)
            full = jnp.where(head == first + j, mm(x, w), 0.0).astype(BF)
            at = i * 1024 + j * 128
            o_ref[:, at : at + 256] = mm(pick, full).astype(BF)


def out_body(v_ref, own_ref, other_ref, o_ref):
    depth = own_ref.shape[1]
    total = mm_t(v_ref[:, :depth], own_ref[...])
    total = total + mm_t(v_ref[:, depth:], other_ref[...])
    o_ref[...] = total.astype(BF)


def mix_body(p_ref, mine_ref, gain_ref, c_ref, o_ref):
    k = iota((32, 256), 1)
    place = ((k >> 1) & 7) * 4 + ((k >> 4) & 1) * 2 + (k & 1)
    pick = (iota((32, 256), 0) == place).astype(BF)
    combined = mine_ref[...].astype(F32) + mm(pick, p_ref[...])
    c_ref[...] = combined
    squares = jnp.sum(combined * combined, axis=1, keepdims=True)
    high = squares.astype(BF).astype(F32)
    lane = iota((32, 512), 1)
    extra = jnp.where(lane == 448, high, jnp.where(lane == 449, squares - high, 0.0))
    extra = extra.astype(BF)
    scaled = (combined * gain_ref[...].astype(F32)).astype(BF)
    for z in range(8):
        o_ref[z] = extra
        o_ref[z, :, :448] = scaled


def units_body(x_ref, own_ref, other_ref, o_ref):
    x = x_ref[:, :448]
    width = own_ref.shape[1]
    step = 768
    for i, w_ref in enumerate((own_ref, other_ref)):
        for j in range(0, width, step):
            at = i * width + j
            o_ref[:, at : at + step] = mm(x, w_ref[:, j : j + step]).astype(BF)
    o_ref[:, 2 * width :] = x_ref[:, 384:]


def gate_body(p_ref, o_ref):
    units = o_ref.shape[2] // 2
    tail = jnp.sum(p_ref[:, :, 4 * units :].astype(F32), axis=0)
    lane = iota(tail.shape, 1)
    tail = jnp.where((lane == 64) | (lane == 65), tail, 0.0)
    factor = lax.rsqrt(jnp.sum(tail, axis=1, keepdims=True) / D + 1e-06)
    step = 384
    for i in range(2):
        for j in range(0, units, step):
            at = 2 * i * units + j
            gate = jnp.sum(p_ref[:, :, at : at + step].astype(F32), axis=0) * factor
            at = at + units
            up = jnp.sum(p_ref[:, :, at : at + step].astype(F32), axis=0) * factor
            hidden = (gate / (1.0 + jnp.exp(-gate)) * up).astype(BF)
            at = i * units + j
            for r in range(16):
                o_ref[r, :, at : at + step] = hidden


def local(
    queries,
    latent_cache,
    lengths,
    counts,
    residual,
    value_up,
    out_proj,
    norm_gain,
    gate_up,
    down_proj,
):
    shape = jax.ShapeDtypeStruct
    core = lax.axis_index("c").reshape(1)
    out_proj = out_proj.T
    down_proj = down_proj.T
    value_up, out_proj, gate_up, down_proj = [
        (w, lax.ppermute(w, "c", [(0, 1), (1, 0)]))
        for w in (value_up, out_proj, gate_up, down_proj)
    ]
    attended = call(
        attend_body,
        shape((8, 2, 16, KL), BF),
        lengths,
        counts,
        jnp.swapaxes(queries, 1, 2),
        jnp.swapaxes(latent_cache, 1, 2),
        smem=2,
    )
    received = exchange(attended, "z").reshape(256, KL)
    values = call(value_body, shape((256, 2048), BF), core, received, *value_up, smem=1)
    values = exchange(values.reshape(16, 16, 2048), GRP).reshape(256, 2048)
    feats = residual.shape[1]
    partial = call(out_body, shape((256, feats), BF), values, *out_proj)
    pieces = exchange(partial.reshape(16, 16, feats), TP).reshape(256, feats)
    mine = lax.dynamic_slice_in_dim(residual, lax.axis_index(TP) * 32, 32, 0)
    combined, packed = call(
        mix_body,
        (shape((32, feats), F32), shape((8, 32, 512), BF)),
        pieces,
        mine,
        norm_gain.reshape(1, feats),
    )
    packed = exchange(packed, "z").reshape(256, 512)
    units = gate_up[0].shape[2]
    terms = call(
        units_body,
        shape((256, 4 * units + 128), BF),
        packed,
        *[w.reshape(feats, 2 * units) for w in gate_up],
    )
    terms = exchange(terms.reshape(16, 16, -1), GRP)
    hidden = call(gate_body, shape((16, 16, 2 * units), BF), terms)
    hidden = exchange(hidden, GRP).reshape(256, 2 * units)
    last = call(out_body, shape((256, feats), BF), hidden, *down_proj)
    last = exchange(last.reshape(8, 32, feats), "z")
    return (combined + jnp.sum(last.astype(F32), axis=0)).astype(BF)


def solution(mesh):
    inner = Mesh(mesh.devices.reshape(4, 4, 8, 2), GRP + TP)
    every = GRP + TP
    placed = (
        P(every, None, None),
        P(every, None, None),
        P(every),
        P(every),
        P(None, GRP),
        P(TP, None, None),
        P(TP, GRP),
        P(GRP),
        P(GRP, None, TP),
        P(TP, GRP),
    )
    return jax.shard_map(
        local, mesh=inner, in_specs=placed, out_specs=P(TP, GRP), check_vma=False
    )
```

time: 187 us -> 166 us (0.89)
  the two profiles are of different devices: /device:TPU:1 before, /device:TPU:2 now
where the time goes in v3:
time: 166 us; the launch traced here: 165 us
  waiting for transfers between devices  63 us (38%)
  blocking collectives  48.4 us (29%)
  starting transfers between devices  28.4 us (17%)
  Pallas kernels  12.1 us (7%)
  local copies, waits for them, and re-layouts  11.9 us (7%)
    all_to_all x5, waiting for transfers between devices, exchange(): return lax.all_to_all(parts, axes, split_axis=0, concat_axis=0, tiled=False)  57.9 us
    all_to_all x2, blocking collectives, exchange(): return lax.all_to_all(parts, axes, split_axis=0, concat_axis=0, tiled=False)  48.4 us
    all_to_all x5, starting transfers between devices, exchange(): return lax.all_to_all(parts, axes, split_axis=0, concat_axis=0, tiled=False)  28.1 us
    pallas_call x7, Pallas kernels, call(): pl.pallas_call(body, out_shape=shapes, in_specs=[pl.BlockSpec(memory_spac...  12.1 us
    unnamed x25, local copies, waits for them, and re-layouts  11.8 us
    ppermute x4, waiting for transfers between devices, local(): lax.ppermute(w, 'c', [(0, 1), (1, 0)])  5.09 us
  transfers between devices with their start and end apart: 9, of which 7 were waited for; matrix products, arithmetic and copies ran while one was open for 3% of the time, Pallas kernels for 5%

profile of v3, /device:TPU:2, one launch (start us, length us, event | category | flops | bytes accessed | tf_op | source)
XLA Modules:
  0.0 165.3 jit_solution(11794668798641599915)
XLA Ops:
  0.0 0.0 copy-start
  0.0 0.0 collective-permute-start
  0.7 0.0 copy-start.2
  0.7 1.3 copy-done.2
  2.0 0.0 copy-start.8
  2.0 1.0 copy-done.8
  2.9 0.0 copy-start.9
  2.9 0.7 copy-done.9
  3.6 0.0 copy-start.3
  3.6 2.3 %shard_map.100 = bf16[8,2,16,512]{3,2,1,0:T(8,128)(2,1)} custom-call(s32[2]{0:T(128)S(1)} %copy-done.9, s32[1]{0:T(128)S(6)} %copy.15.counts, bf16[2,576,128]{2,1,0:T(8,128)(2,1)S(1)} %bitcast.32, bf16[2,576,512]{2,1,0:T(8,128)(2,1)S(1)} %bitcast.23), custom_call_target="tpu_custom_call" | custom-call | tf_op jit(solution)/shard_map/pallas_call | solution.py:22
  5.9 8.5 %all-to-all-start = ((bf16[8,2,16,512]{3,2,1,0:T(8,128)(2,1)}), bf16[8,2,16,512]{3,2,1,0:T(8,128)(2,1)S(1)}, u32[]{:S(2)}, u32[]{:S(2)}) async-start(bf16[8,2,16,512]{3,2,1,0:T(8,128)(2,1)} %shard_map.100), calls=%async_computation | async-start | bytes 524288 | tf_op jit(solution)/shard_map/all_to_all | solution.py:18
  14.3 0.2 collective-permute-start.2
  14.5 12.3 %all-to-all-done = bf16[8,2,16,512]{3,2,1,0:T(8,128)(2,1)S(1)} async-done(((bf16[8,2,16,512]{3,2,1,0:T(8,128)(2,1)}), bf16[8,2,16,512]{3,2,1,0:T(8,128)(2,1)S(1)}, u32[]{:S(2)}, u32[]{:S(2)}) %all-to-all-start) | async-done | bytes 262176 | tf_op jit(solution)/shard_map/all_to_all | solution.py:18
  26.8 0.0 collective-permute-done.other_ref
  26.8 0.0 copy-done.3
  26.8 3.7 %shard_map.101 = bf16[256,2048]{1,0:T(8,128)(2,1)} custom-call(s32[1]{0:T(128)} %bitcast.core, bf16[256,512]{1,0:T(8,128)(2,1)S(1)} %bitcast.24, bf16[8,512,128]{2,1,0:T(8,128)(2,1)S(1)} %copy-done.3, bf16[8,512,128]{2,1,0:T(8,128)(2,1)S(1)} %collective-permute-done.other_ref), custom_call_target="tpu_custom_call" | custom-call | tf_op jit(solution)/shard_map/pallas_call | solution.py:22
  30.5 0.0 copy-start.7
  30.5 7.6 %all-to-all-start.1 = ((bf16[16,16,2048]{2,1,0:T(8,128)(2,1)}), bf16[16,16,2048]{2,1,0:T(8,128)(2,1)S(1)}, u32[]{:S(2)}, u32[]{:S(2)}) async-start(bf16[16,16,2048]{2,1,0:T(8,128)(2,1)} %bitcast.4), calls=%async_computation.1 | async-start | bytes 2097152 | tf_op jit(solution)/shard_map/all_to_all | solution.py:18
  38.1 0.0 copy-start.10
  38.1 0.0 copy-done.7
  38.2 0.1 collective-permute-start.1
  38.3 2.5 %collective-permute-done.1.other_ref = bf16[448,1024]{1,0:T(8,128)(2,1)S(1)} collective-permute-done((bf16[448,1024]{1,0:T(8,128)(2,1)S(1)}, bf16[448,1024]{1,0:T(8,128)(2,1)S(1)}, u32[]{:S(2)}, u32[]{:S(2)}) %collective-permute-start.1) | collective-permute-done | bytes 917536 | tf_op jit(solution)/shard_map/ppermute | solution.py:141
  40.7 13.4 %all-to-all-done.1 = bf16[16,16,2048]{2,1,0:T(8,128)(2,1)S(1)} async-done(((bf16[16,16,2048]{2,1,0:T(8,128)(2,1)}), bf16[16,16,2048]{2,1,0:T(8,128)(2,1)S(1)}, u32[]{:S(2)}, u32[]{:S(2)}) %all-to-all-start.1) | async-done | bytes 1048608 | tf_op jit(solution)/shard_map/all_to_all | solution.py:18
  54.1 1.4 shard_map.102
  55.6 3.5 %all-to-all-start.2 = ((bf16[16,16,448]{2,1,0:T(8,128)(2,1)}), bf16[16,16,448]{2,1,0:T(8,128)(2,1)S(1)}, u32[]{:S(2)}, u32[]{:S(2)}) async-start(bf16[16,16,448]{2,1,0:T(8,128)(2,1)} %bitcast.7), calls=%async_computation.2 | async-start | bytes 524288 | tf_op jit(solution)/shard_map/all_to_all | solution.py:18
  59.1 0.0 copy-done
  59.1 0.1 constant_dynamic-slice_fusion
  59.2 0.1 copy.12.mine_ref
  59.3 0.0 copy-done.10
  59.3 10.8 %all-to-all-done.2 = bf16[16,16,448]{2,1,0:T(8,128)(2,1)S(1)} async-done(((bf16[16,16,448]{2,1,0:T(8,128)(2,1)}), bf16[16,16,448]{2,1,0:T(8,128)(2,1)S(1)}, u32[]{:S(2)}, u32[]{:S(2)}) %all-to-all-start.2) | async-done | bytes 229408 | tf_op jit(solution)/shard_map/all_to_all | solution.py:18
  70.1 1.0 shard_map.103
  71.1 3.4 %all-to-all-start.3 = ((bf16[8,32,512]{2,1,0:T(8,128)(2,1)}), bf16[8,32,512]{2,1,0:T(8,128)(2,1)S(1)}, u32[]{:S(2)}, u32[]{:S(2)}) async-start(bf16[8,32,512]{2,1,0:T(8,128)(2,1)} %get-tuple-element.8), calls=%async_computation.3 | async-start | bytes 524288 | tf_op jit(solution)/shard_map/all_to_all | solution.py:18
  74.5 1.9 %copy.13 = bf16[56,8,2,1152]{3,1,2,0:T(8,128)(2,1)S(1)} copy(bf16[56,8,2,1152]{3,2,1,0:T(2,128)(2,1)} %bitcast.33) | data formatting | bytes 4128768
  76.4 0.0 collective-permute-done.2
  76.4 3.2 %copy.14 = bf16[56,8,2,1152]{3,1,2,0:T(8,128)(2,1)} copy(bf16[56,8,2,1152]{3,2,1,0:T(2,128)(2,1)} %bitcast.16) | data formatting | bytes 4128768
  79.6 8.2 %all-to-all-done.3 = bf16[8,32,512]{2,1,0:T(8,128)(2,1)S(1)} async-done(((bf16[8,32,512]{2,1,0:T(8,128)(2,1)}), bf16[8,32,512]{2,1,0:T(8,128)(2,1)S(1)}, u32[]{:S(2)}, u32[]{:S(2)}) %all-to-all-start.3) | async-done | bytes 262176 | tf_op jit(solution)/shard_map/all_to_all | solution.py:18
  87.8 0.0 copy-start.1
  87.8 1.6 copy-done.1
  89.3 1.4 shard_map.104
  90.7 35.5 %all_to_all.35.p_ref = bf16[16,16,4736]{2,1,0:T(8,128)(2,1)S(1)} all-to-all(bf16[16,16,4736]{2,1,0:T(8,128)(2,1)S(1)} %bitcast.18), channel_id=1, replica_groups=mesh['y'=4,'x'=4,'z'=8,'c'=2] {'y','x'}, dimensions={0} | all-to-all | bytes 4849664 | tf_op jit(solution)/shard_map/all_to_all | solution.py:18
  126.3 1.4 shard_map.105
  127.7 0.0 copy-start.4
  127.7 5.1 %all-to-all-start.5 = ((bf16[16,16,2304]{2,1,0:T(8,128)(2,1)}), bf16[16,16,2304]{2,1,0:T(8,128)(2,1)S(1)}, u32[]{:S(2)}, u32[]{:S(2)}) async-start(bf16[16,16,2304]{2,1,0:T(8,128)(2,1)} %shard_map.105), calls=%async_computation.5 | async-start | bytes 2359296 | tf_op jit(solution)/shard_map/all_to_all | solution.py:18
  132.8 0.0 copy-done.4
  132.8 0.1 collective-permute-start.3
  132.9 2.6 %collective-permute-done.3.other_ref = bf16[448,1152]{1,0:T(8,128)(2,1)S(1)} collective-permute-done((bf16[448,1152]{1,0:T(8,128)(2,1)S(1)}, bf16[448,1152]{1,0:T(8,128)(2,1)S(1)}, u32[]{:S(2)}, u32[]{:S(2)}) %collective-permute-start.3) | collective-permute-done | bytes 1032224 | tf_op jit(solution)/shard_map/ppermute | solution.py:141
  135.5 0.0 copy-start.5
  135.5 1.0 copy-done.5
  136.5 13.2 %all-to-all-done.5 = bf16[16,16,2304]{2,1,0:T(8,128)(2,1)S(1)} async-done(((bf16[16,16,2304]{2,1,0:T(8,128)(2,1)}), bf16[16,16,2304]{2,1,0:T(8,128)(2,1)S(1)}, u32[]{:S(2)}, u32[]{:S(2)}) %all-to-all-start.5) | async-done | bytes 1179680 | tf_op jit(solution)/shard_map/all_to_all | solution.py:18
  149.7 0.0 copy-start.6
  149.7 1.2 copy-done.6
  150.9 0.9 shard_map.106
  151.7 12.9 %all_to_all.36 = bf16[8,32,448]{2,1,0:T(8,128)(2,1)S(1)} all-to-all(bf16[8,32,448]{2,1,0:T(8,128)(2,1)S(1)} %bitcast.26), channel_id=1, replica_groups=mesh['y'=4,'x'=4,'z'=8,'c'=2] {'z'}, dimensions={0} | all-to-all | bytes 458752 | tf_op jit(solution)/shard_map/all_to_all | solution.py:18
  164.7 0.6 add_convert_fusion
  (2 shorter events, 0.0 us)
Async XLA Ops:
  0.0 59.1 %copy-start = (bf16[512,448]{0,1:T(8,128)(2,1)S(1)}, bf16[512,448]{0,1:T(8,128)(2,1)}, u32[]{:S(2)}) copy-start(bf16[512,448]{0,1:T(8,128)(2,1)} %param.14) | copy-start | bytes 1376260
  0.0 26.8 %collective-permute-start = (bf16[8,512,128]{2,1,0:T(8,128)(2,1)}, bf16[8,512,128]{2,1,0:T(8,128)(2,1)S(1)}, u32[]{:S(2)}, u32[]{:S(2)}) collective-permute-start(bf16[8,512,128]{2,1,0:T(8,128)(2,1)} %own_ref.1), channel_id=1, source_target_pairs={{0,1},{1,0},{2,3},{3,2},{4,5},{5,4},{6,7},{7,6},{8,9},{9,8},{10,11... | collective-permute-start | bytes 3145736 | tf_op jit(solution)/shard_map/ppermute | solution.py:141
  0.7 1.3 copy-start.2
  2.0 1.0 copy-start.8
  2.9 0.7 copy-start.9
  3.6 23.2 %copy-start.3 = (bf16[8,512,128]{2,1,0:T(8,128)(2,1)S(1)}, bf16[8,512,128]{2,1,0:T(8,128)(2,1)}, u32[]{:S(2)}) copy-start(bf16[8,512,128]{2,1,0:T(8,128)(2,1)} %own_ref.1) | copy-start | bytes 3145732
  5.9 21.0 %all-to-all-start = ((bf16[8,2,16,512]{3,2,1,0:T(8,128)(2,1)}), bf16[8,2,16,512]{3,2,1,0:T(8,128)(2,1)S(1)}, u32[]{:S(2)}, u32[]{:S(2)}) async-start(bf16[8,2,16,512]{3,2,1,0:T(8,128)(2,1)} %shard_map.100), calls=%async_computation | async-start | bytes 524288 | tf_op jit(solution)/shard_map/all_to_all | solution.py:18
  14.3 62.0 %collective-permute-start.2 = (bf16[448,2,1152]{2,1,0:T(2,128)(2,1)}, bf16[448,2,1152]{2,1,0:T(2,128)(2,1)}, u32[]{:S(2)}, u32[]{:S(2)}) collective-permute-start(bf16[448,2,1152]{2,1,0:T(2,128)(2,1)} %param.18), channel_id=1, source_target_pairs={{0,1},{1,0},{2,3},{3,2},{4,5},{5,4},{6,7},{7,6},{8,9},{9,8},{10,11... | collective-permute-start | bytes 6193160 | tf_op jit(solution)/shard_map/ppermute | solution.py:141
  30.5 7.6 %copy-start.7 = (bf16[1024,448]{0,1:T(8,128)(2,1)S(1)}, bf16[1024,448]{0,1:T(8,128)(2,1)}, u32[]{:S(2)}) copy-start(bf16[1024,448]{0,1:T(8,128)(2,1)} %param.16) | copy-start | bytes 2752516
  30.5 23.6 %all-to-all-start.1 = ((bf16[16,16,2048]{2,1,0:T(8,128)(2,1)}), bf16[16,16,2048]{2,1,0:T(8,128)(2,1)S(1)}, u32[]{:S(2)}, u32[]{:S(2)}) async-start(bf16[16,16,2048]{2,1,0:T(8,128)(2,1)} %bitcast.4), calls=%async_computation.1 | async-start | bytes 2097152 | tf_op jit(solution)/shard_map/all_to_all | solution.py:18
  38.1 21.2 %copy-start.10 = (bf16[448]{0:T(512)(128)(2,1)S(1)}, bf16[448]{0:T(512)(128)(2,1)}, u32[]{:S(2)}) copy-start(bf16[448]{0:T(512)(128)(2,1)} %param.17) | copy-start | bytes 2692
  38.2 2.6 %collective-permute-start.1 = (bf16[448,1024]{1,0:T(8,128)(2,1)S(1)}, bf16[448,1024]{1,0:T(8,128)(2,1)S(1)}, u32[]{:S(2)}, u32[]{:S(2)}) collective-permute-start(bf16[448,1024]{1,0:T(8,128)(2,1)S(1)} %bitcast.30), channel_id=1, source_target_pairs={{0,1},{1,0},{2,3},{3,2},{4,5},{5,4},{6,7},{7,6},{8,9},{9,8},{10,11... | collective-permute-start | bytes 2752520 | tf_op jit(solution)/shard_map/ppermute | solution.py:141
  55.6 14.5 %all-to-all-start.2 = ((bf16[16,16,448]{2,1,0:T(8,128)(2,1)}), bf16[16,16,448]{2,1,0:T(8,128)(2,1)S(1)}, u32[]{:S(2)}, u32[]{:S(2)}) async-start(bf16[16,16,448]{2,1,0:T(8,128)(2,1)} %bitcast.7), calls=%async_computation.2 | async-start | bytes 524288 | tf_op jit(solution)/shard_map/all_to_all | solution.py:18
  71.1 16.7 %all-to-all-start.3 = ((bf16[8,32,512]{2,1,0:T(8,128)(2,1)}), bf16[8,32,512]{2,1,0:T(8,128)(2,1)S(1)}, u32[]{:S(2)}, u32[]{:S(2)}) async-start(bf16[8,32,512]{2,1,0:T(8,128)(2,1)} %get-tuple-element.8), calls=%async_computation.3 | async-start | bytes 524288 | tf_op jit(solution)/shard_map/all_to_all | solution.py:18
  87.8 1.6 copy-start.1
  127.7 5.1 %copy-start.4 = (bf16[1152,448]{0,1:T(8,128)(2,1)S(1)}, bf16[1152,448]{0,1:T(8,128)(2,1)}, u32[]{:S(2)}) copy-start(bf16[1152,448]{0,1:T(8,128)(2,1)} %param.19) | copy-start | bytes 3096580
  127.7 21.9 %all-to-all-start.5 = ((bf16[16,16,2304]{2,1,0:T(8,128)(2,1)}), bf16[16,16,2304]{2,1,0:T(8,128)(2,1)S(1)}, u32[]{:S(2)}, u32[]{:S(2)}) async-start(bf16[16,16,2304]{2,1,0:T(8,128)(2,1)} %shard_map.105), calls=%async_computation.5 | async-start | bytes 2359296 | tf_op jit(solution)/shard_map/all_to_all | solution.py:18
  132.8 2.7 %collective-permute-start.3 = (bf16[448,1152]{1,0:T(8,128)(2,1)S(1)}, bf16[448,1152]{1,0:T(8,128)(2,1)S(1)}, u32[]{:S(2)}, u32[]{:S(2)}) collective-permute-start(bf16[448,1152]{1,0:T(8,128)(2,1)S(1)} %bitcast.28), channel_id=1, source_target_pairs={{0,1},{1,0},{2,3},{3,2},{4,5},{5,4},{6,7},{7,6},{8,9},{9,8},{10,11... | collective-permute-start | bytes 3096584 | tf_op jit(solution)/shard_map/ppermute | solution.py:141
  135.5 1.0 copy-start.5
  149.7 1.2 copy-start.6

commit v4 on v3

--- a/solution.py
+++ b/solution.py
@@ -10,22 +10,29 @@
 QKD = 192
 GRP = ("y", "x")
 TP = ("z", "c")
+XYC = ("y", "x", "c")
+LINES_X = [[[8 * y + 2 * x + c for x in range(4)] for y in range(4)] for c in range(2)]
+LINES_Y = [[[8 * y + 2 * x + c for y in range(4)] for x in range(4)] for c in range(2)]
+FIRST = LINES_X[0] + LINES_Y[1]
+SECOND = LINES_Y[0] + LINES_X[1]
 BF = jnp.bfloat16
 F32 = jnp.float32
 
 
-def exchange(parts, axes):
-    return lax.all_to_all(parts, axes, split_axis=0, concat_axis=0, tiled=False)
-
-
-def call(body, shapes, *args, smem=0, limit=40):
+def exchange(parts, axes, groups=None):
+    return lax.all_to_all(
+        parts, axes, split_axis=0, concat_axis=0, axis_index_groups=groups
+    )
+
+
+def call(body, shapes, *args, smem=0, any_space=0, scratch=(), limit=8):
+    spaces = [pltpu.SMEM] * smem + [pltpu.HBM] * any_space
+    spaces = spaces + [pltpu.VMEM] * (len(args) - len(spaces))
     return pl.pallas_call(
         body,
         out_shape=shapes,
-        in_specs=[
-            pl.BlockSpec(memory_space=pltpu.SMEM if i < smem else pltpu.VMEM)
-            for i in range(len(args))
-        ],
+        in_specs=[pl.BlockSpec(memory_space=space) for space in spaces],
+        scratch_shapes=scratch,
         compiler_params=pltpu.CompilerParams(vmem_limit_bytes=limit * 2**20),
     )(*args)
 
@@ -42,9 +49,26 @@
     return lax.dot_general(a, b, (((1,), (1,)), ((), ())), preferred_element_type=F32)
 
 
-def attend_body(lengths, counts, q_ref, c_ref, o_ref):
+def attend_body(len_hbm, cnt_hbm, q_hbm, c_hbm, o_ref, lengths, counts, q_ref, c_ref, sems):
+    copies = [
+        pltpu.make_async_copy(len_hbm, lengths, sems.at[0]),
+        pltpu.make_async_copy(cnt_hbm, counts, sems.at[1]),
+    ]
     for slot in range(2):
+        copies.append(
+            pltpu.make_async_copy(q_hbm.at[slot], q_ref.at[slot], sems.at[2 + 2 * slot])
+        )
+        copies.append(
+            pltpu.make_async_copy(c_hbm.at[slot], c_ref.at[slot], sems.at[3 + 2 * slot])
+        )
+    for copy in copies:
+        copy.start()
+    copies[0].wait()
+    copies[1].wait()
+    for slot in range(2):
+        copies[2 + 2 * slot].wait()
         query = q_ref[slot].T
+        copies[3 + 2 * slot].wait()
         scores = mm(query, c_ref[slot]) * QKD ** (-0.5)
         scores = jnp.where(iota(scores.shape, 1) < lengths[slot], scores, -jnp.inf)
         expo = jnp.exp(scores - jnp.max(scores, axis=1, keepdims=True))
@@ -55,16 +79,16 @@
 
 
 def value_body(core, x_ref, own_ref, other_ref, o_ref):
-    x = x_ref[...]
-    pick = ((iota((256, 256), 0) & 15) == (iota((256, 256), 1) >> 4)).astype(BF)
-    head = (iota((256, 256), 0) & 15) - (iota((256, 256), 1) >> 7)
+    at = iota((256, 256), 0)
+    source = (at & 15) * 16 + ((at >> 4) ^ (8 * core[0]))
+    pick = (iota((256, 256), 1) == source).astype(BF)
+    x = mm(pick, x_ref[...]).astype(BF)
     for i, w_ref in enumerate((own_ref, other_ref)):
-        first = 8 * (core[0] if i == 0 else 1 - core[0])
-        for j in range(0, 8, 2):
-            w = jnp.concatenate([w_ref[j], w_ref[j + 1]], axis=1)
-            full = jnp.where(head == first + j, mm(x, w), 0.0).astype(BF)
-            at = i * 1024 + j * 128
-            o_ref[:, at : at + 256] = mm(pick, full).astype(BF)
+        for h in range(8):
+            k = 8 * i + h
+            value = mm(x[16 * k : 16 * k + 16], w_ref[h]).astype(BF)
+            for r in range(16):
+                o_ref[16 * r : 16 * r + 16, 128 * k : 128 * k + 128] = value
 
 
 def out_body(v_ref, own_ref, other_ref, o_ref):
@@ -91,15 +115,36 @@
         o_ref[z, :, :448] = scaled
 
 
-def units_body(x_ref, own_ref, other_ref, o_ref):
-    x = x_ref[:, :448]
+def units_body(core, x_ref, own_ref, other_ref, o_ref, rows_ref):
+    for i in range(4):
+        for j in range(4):
+            block = jnp.where(core[0] == 0, 4 * j + i, 4 * i + j)
+            at = pl.multiple_of(block * 16, 16)
+            to = 16 * (4 * i + j)
+            rows_ref[to : to + 16] = x_ref[pl.ds(at, 16)]
+    x = rows_ref[:, :448]
     width = own_ref.shape[1]
     step = 768
     for i, w_ref in enumerate((own_ref, other_ref)):
         for j in range(0, width, step):
             at = i * width + j
             o_ref[:, at : at + step] = mm(x, w_ref[:, j : j + step]).astype(BF)
-    o_ref[:, 2 * width :] = x_ref[:, 384:]
+    o_ref[:, 2 * width :] = rows_ref[:, 384:]
+
+
+def half_body(p_ref, o_ref):
+    width = o_ref.shape[1] - 128
+    step = width // 6
+    for j in range(0, width, step):
+        part = p_ref[:, :, j : j + step].astype(F32)
+        o_ref[:, j : j + step] = jnp.sum(part, axis=0).astype(BF)
+    tail = jnp.sum(p_ref[:, :, width:].astype(F32), axis=0)
+    lane = iota(tail.shape, 1)
+    tail = jnp.where((lane == 64) | (lane == 65), tail, 0.0)
+    squares = jnp.sum(tail, axis=1, keepdims=True)
+    high = squares.astype(BF).astype(F32)
+    tail = jnp.where(lane == 64, high, jnp.where(lane == 65, squares - high, 0.0))
+    o_ref[:, width:] = tail.astype(BF)
 
 
 def gate_body(p_ref, o_ref):
@@ -148,7 +193,15 @@
         counts,
         jnp.swapaxes(queries, 1, 2),
         jnp.swapaxes(latent_cache, 1, 2),
-        smem=2,
+        any_space=4,
+        scratch=[
+            pltpu.SMEM((2,), jnp.int32),
+            pltpu.SMEM((1,), jnp.int32),
+            pltpu.VMEM((2, 576, 128), BF),
+            pltpu.VMEM((2, 576, 512), BF),
+            pltpu.SemaphoreType.DMA((6,)),
+        ],
+        limit=60,
     )
     received = exchange(attended, "z").reshape(256, KL)
     values = call(value_body, shape((256, 2048), BF), core, received, *value_up, smem=1)
@@ -169,10 +222,15 @@
     terms = call(
         units_body,
         shape((256, 4 * units + 128), BF),
+        core,
         packed,
         *[w.reshape(feats, 2 * units) for w in gate_up],
-    )
-    terms = exchange(terms.reshape(16, 16, -1), GRP)
+        smem=1,
+        scratch=[pltpu.VMEM((256, 512), BF)],
+    )
+    terms = exchange(terms.reshape(4, 64, -1), XYC, FIRST)
+    terms = call(half_body, shape(terms.shape[1:], BF), terms)
+    terms = exchange(terms.reshape(4, 16, -1), XYC, SECOND)
     hidden = call(gate_body, shape((16, 16, 2 * units), BF), terms)
     hidden = exchange(hidden, GRP).reshape(256, 2 * units)
     last = call(out_body, shape((256, feats), BF), hidden, *down_proj)

time: 166 us -> 158 us (0.952)
  blocking collectives: 48.4 us -> 45 us
  local copies, waits for them, and re-layouts: 11.9 us -> 9.02 us
    all_to_all x2 -> x3, blocking collectives: 48.4 us -> 45 us  [exchange(): lax.all_to_all(parts, axes, split_axis=0, concat_axis=0, axis_index_group...]
    unnamed x25 -> x19, local copies, waits for them, and re-layouts: 11.8 us -> 8.91 us
    pallas_call x7 -> x8, Pallas kernels: 12.1 us -> 11.1 us  [call(): pl.pallas_call(body, out_shape=shapes, in_specs=[pl.BlockSpec(memory_spac...]
where the time goes in v4:
time: 158 us; the launch traced here: 157 us
  waiting for transfers between devices  62.5 us (40%)
  blocking collectives  45 us (28%)
  starting transfers between devices  28.3 us (18%)
  Pallas kernels  11.1 us (7%)
  local copies, waits for them, and re-layouts  9.02 us (6%)
    all_to_all x5, waiting for transfers between devices, exchange(): lax.all_to_all(parts, axes, split_axis=0, concat_axis=0, axis_index_group...  57.4 us
    all_to_all x3, blocking collectives, exchange(): lax.all_to_all(parts, axes, split_axis=0, concat_axis=0, axis_index_group...  45 us
    all_to_all x5, starting transfers between devices, exchange(): lax.all_to_all(parts, axes, split_axis=0, concat_axis=0, axis_index_group...  28 us
    pallas_call x8, Pallas kernels, call(): pl.pallas_call(body, out_shape=shapes, in_specs=[pl.BlockSpec(memory_spac...  11.1 us
    unnamed x19, local copies, waits for them, and re-layouts  8.91 us
    ppermute x4, waiting for transfers between devices, local(): lax.ppermute(w, 'c', [(0, 1), (1, 0)])  5.09 us
  transfers between devices with their start and end apart: 9, of which 7 were waited for; matrix products, arithmetic and copies ran while one was open for 3% of the time, Pallas kernels for 5%

profile of v4, /device:TPU:2, one launch (start us, length us, event | category | flops | bytes accessed | tf_op | source)
XLA Modules:
  0.0 157.4 jit_solution(17533368747862338295)
XLA Ops:
  0.0 0.0 copy-start
  0.0 0.0 copy-start.2
  0.0 0.0 collective-permute-start
  0.8 3.2 %shard_map.100 = bf16[8,2,16,512]{3,2,1,0:T(8,128)(2,1)} custom-call(s32[2]{0:T(128)} %len_hbm.1, s32[1]{0:T(128)S(6)} %copy.15.cnt_hbm, bf16[2,576,128]{2,1,0:T(8,128)(2,1)} %bitcast.35, bf16[2,576,512]{2,1,0:T(8,128)(2,1)} %bitcast.34), custom_call_target="tpu_custom_call" | custom-call | tf_op jit(solution)/shard_map/pallas_call | solution.py:31
  3.9 8.5 %all-to-all-start = ((bf16[8,2,16,512]{3,2,1,0:T(8,128)(2,1)}), bf16[8,2,16,512]{3,2,1,0:T(8,128)(2,1)S(1)}, u32[]{:S(2)}, u32[]{:S(2)}) async-start(bf16[8,2,16,512]{3,2,1,0:T(8,128)(2,1)} %shard_map.100), calls=%async_computation | async-start | bytes 524288 | tf_op jit(solution)/shard_map/all_to_all | solution.py:23
  12.4 0.1 collective-permute-start.2
  12.5 12.3 %all-to-all-done = bf16[8,2,16,512]{3,2,1,0:T(8,128)(2,1)S(1)} async-done(((bf16[8,2,16,512]{3,2,1,0:T(8,128)(2,1)}), bf16[8,2,16,512]{3,2,1,0:T(8,128)(2,1)S(1)}, u32[]{:S(2)}, u32[]{:S(2)}) %all-to-all-start) | async-done | bytes 262176 | tf_op jit(solution)/shard_map/all_to_all | solution.py:23
  24.9 0.0 collective-permute-done.other_ref
  24.9 0.0 copy-done.2
  24.9 1.6 %shard_map.101 = bf16[256,2048]{1,0:T(8,128)(2,1)} custom-call(s32[1]{0:T(128)} %bitcast.core, bf16[256,512]{1,0:T(8,128)(2,1)S(1)} %bitcast.25, bf16[8,512,128]{2,1,0:T(8,128)(2,1)S(1)} %copy-done.2, bf16[8,512,128]{2,1,0:T(8,128)(2,1)S(1)} %collective-permute-done.other_ref), custom_call_target="tpu_custom_call" | custom-call | tf_op jit(solution)/shard_map/pallas_call | solution.py:31
  26.5 0.0 copy-start.6
  26.5 7.6 %all-to-all-start.1 = ((bf16[16,16,2048]{2,1,0:T(8,128)(2,1)}), bf16[16,16,2048]{2,1,0:T(8,128)(2,1)S(1)}, u32[]{:S(2)}, u32[]{:S(2)}) async-start(bf16[16,16,2048]{2,1,0:T(8,128)(2,1)} %bitcast.4), calls=%async_computation.1 | async-start | bytes 2097152 | tf_op jit(solution)/shard_map/all_to_all | solution.py:23
  34.1 0.0 copy-start.7
  34.1 0.0 copy-done.6
  34.1 0.1 collective-permute-start.1
  34.2 2.5 %collective-permute-done.1.other_ref = bf16[448,1024]{1,0:T(8,128)(2,1)S(1)} collective-permute-done((bf16[448,1024]{1,0:T(8,128)(2,1)S(1)}, bf16[448,1024]{1,0:T(8,128)(2,1)S(1)}, u32[]{:S(2)}, u32[]{:S(2)}) %collective-permute-start.1) | collective-permute-done | bytes 917536 | tf_op jit(solution)/shard_map/ppermute | solution.py:186
  36.6 13.3 %all-to-all-done.1 = bf16[16,16,2048]{2,1,0:T(8,128)(2,1)S(1)} async-done(((bf16[16,16,2048]{2,1,0:T(8,128)(2,1)}), bf16[16,16,2048]{2,1,0:T(8,128)(2,1)S(1)}, u32[]{:S(2)}, u32[]{:S(2)}) %all-to-all-start.1) | async-done | bytes 1048608 | tf_op jit(solution)/shard_map/all_to_all | solution.py:23
  50.0 1.4 shard_map.102
  51.4 3.5 %all-to-all-start.2 = ((bf16[16,16,448]{2,1,0:T(8,128)(2,1)}), bf16[16,16,448]{2,1,0:T(8,128)(2,1)S(1)}, u32[]{:S(2)}, u32[]{:S(2)}) async-start(bf16[16,16,448]{2,1,0:T(8,128)(2,1)} %bitcast.7), calls=%async_computation.2 | async-start | bytes 524288 | tf_op jit(solution)/shard_map/all_to_all | solution.py:23
  55.0 0.0 copy-done
  55.0 0.1 constant_dynamic-slice_fusion
  55.1 0.1 copy.12.mine_ref
  55.2 0.0 copy-done.7
  55.2 10.8 %all-to-all-done.2 = bf16[16,16,448]{2,1,0:T(8,128)(2,1)S(1)} async-done(((bf16[16,16,448]{2,1,0:T(8,128)(2,1)}), bf16[16,16,448]{2,1,0:T(8,128)(2,1)S(1)}, u32[]{:S(2)}, u32[]{:S(2)}) %all-to-all-start.2) | async-done | bytes 229408 | tf_op jit(solution)/shard_map/all_to_all | solution.py:23
  66.0 1.0 shard_map.103
  66.9 3.4 %all-to-all-start.3 = ((bf16[8,32,512]{2,1,0:T(8,128)(2,1)}), bf16[8,32,512]{2,1,0:T(8,128)(2,1)S(1)}, u32[]{:S(2)}, u32[]{:S(2)}) async-start(bf16[8,32,512]{2,1,0:T(8,128)(2,1)} %get-tuple-element.8), calls=%async_computation.3 | async-start | bytes 524288 | tf_op jit(solution)/shard_map/all_to_all | solution.py:23
  70.3 1.9 %copy.13 = bf16[56,8,2,1152]{3,1,2,0:T(8,128)(2,1)S(1)} copy(bf16[56,8,2,1152]{3,2,1,0:T(2,128)(2,1)} %bitcast.33) | data formatting | bytes 4128768
  72.2 0.0 collective-permute-done.2
  72.2 3.2 %copy.14 = bf16[56,8,2,1152]{3,1,2,0:T(8,128)(2,1)} copy(bf16[56,8,2,1152]{3,2,1,0:T(2,128)(2,1)} %bitcast.17) | data formatting | bytes 4128768
  75.4 8.2 %all-to-all-done.3 = bf16[8,32,512]{2,1,0:T(8,128)(2,1)S(1)} async-done(((bf16[8,32,512]{2,1,0:T(8,128)(2,1)}), bf16[8,32,512]{2,1,0:T(8,128)(2,1)S(1)}, u32[]{:S(2)}, u32[]{:S(2)}) %all-to-all-start.3) | async-done | bytes 262176 | tf_op jit(solution)/shard_map/all_to_all | solution.py:23
  83.6 0.0 copy-start.1
  83.6 1.6 %copy-done.1 = bf16[56,8,2,1152]{3,1,2,0:T(8,128)(2,1)S(1)} copy-done((bf16[56,8,2,1152]{3,1,2,0:T(8,128)(2,1)S(1)}, bf16[56,8,2,1152]{3,1,2,0:T(8,128)(2,1)}, u32[]{:S(2)}) %copy-start.1) | copy-done | bytes 2064408
  85.2 1.4 shard_map.104
  86.6 21.2 %all_to_all.40.p_ref = bf16[4,64,4736]{2,1,0:T(8,128)(2,1)S(1)} all-to-all(bf16[4,64,4736]{2,1,0:T(8,128)(2,1)S(1)} %bitcast.19), channel_id=1, replica_groups={{0,16,32,48},{64,80,96,112},{128,144,160,176},{192,208,224,240},{1,65,1..., dimensions={0} | all-to-all | bytes 4849664 | tf_op jit(solution)/shard_map/all_to_all | solution.py:23
  107.8 0.4 shard_map.105
  108.2 10.9 %all_to_all.41.p_ref = bf16[4,16,4736]{2,1,0:T(8,128)(2,1)S(1)} all-to-all(bf16[4,16,4736]{2,1,0:T(8,128)(2,1)S(1)} %bitcast.24), channel_id=1, replica_groups={{0,64,128,192},{16,80,144,208},{32,96,160,224},{48,112,176,240},{1,17,3..., dimensions={0} | all-to-all | bytes 1212416 | tf_op jit(solution)/shard_map/all_to_all | solution.py:23
  119.1 0.0 copy-start.3
  119.1 1.3 shard_map.106
  120.4 4.9 %all-to-all-start.6 = ((bf16[16,16,2304]{2,1,0:T(8,128)(2,1)}), bf16[16,16,2304]{2,1,0:T(8,128)(2,1)S(1)}, u32[]{:S(2)}, u32[]{:S(2)}) async-start(bf16[16,16,2304]{2,1,0:T(8,128)(2,1)} %shard_map.106), calls=%async_computation.6 | async-start | bytes 2359296 | tf_op jit(solution)/shard_map/all_to_all | solution.py:23
  125.3 0.0 copy-done.3
  125.3 0.1 collective-permute-start.3
  125.5 2.6 %collective-permute-done.3.other_ref = bf16[448,1152]{1,0:T(8,128)(2,1)S(1)} collective-permute-done((bf16[448,1152]{1,0:T(8,128)(2,1)S(1)}, bf16[448,1152]{1,0:T(8,128)(2,1)S(1)}, u32[]{:S(2)}, u32[]{:S(2)}) %collective-permute-start.3) | collective-permute-done | bytes 1032224 | tf_op jit(solution)/shard_map/ppermute | solution.py:186
  128.1 0.0 copy-start.4
  128.1 0.9 copy-done.4
  129.0 12.8 %all-to-all-done.6 = bf16[16,16,2304]{2,1,0:T(8,128)(2,1)S(1)} async-done(((bf16[16,16,2304]{2,1,0:T(8,128)(2,1)}), bf16[16,16,2304]{2,1,0:T(8,128)(2,1)S(1)}, u32[]{:S(2)}, u32[]{:S(2)}) %all-to-all-start.6) | async-done | bytes 1179680 | tf_op jit(solution)/shard_map/all_to_all | solution.py:23
  141.8 0.0 copy-start.5
  141.8 1.2 copy-done.5
  143.0 0.9 shard_map.107
  143.9 12.9 %all_to_all.42 = bf16[8,32,448]{2,1,0:T(8,128)(2,1)S(1)} all-to-all(bf16[8,32,448]{2,1,0:T(8,128)(2,1)S(1)} %bitcast.28), channel_id=1, replica_groups=mesh['y'=4,'x'=4,'z'=8,'c'=2] {'z'}, dimensions={0} | all-to-all | bytes 458752 | tf_op jit(solution)/shard_map/all_to_all | solution.py:23
  156.8 0.6 add_convert_fusion
  (2 shorter events, 0.0 us)
Async XLA Ops:
  0.0 55.0 %copy-start = (bf16[512,448]{0,1:T(8,128)(2,1)S(1)}, bf16[512,448]{0,1:T(8,128)(2,1)}, u32[]{:S(2)}) copy-start(bf16[512,448]{0,1:T(8,128)(2,1)} %param.14) | copy-start | bytes 1376260
  0.0 24.9 %copy-start.2 = (bf16[8,512,128]{2,1,0:T(8,128)(2,1)S(1)}, bf16[8,512,128]{2,1,0:T(8,128)(2,1)}, u32[]{:S(2)}) copy-start(bf16[8,512,128]{2,1,0:T(8,128)(2,1)} %own_ref.1) | copy-start | bytes 3145732
  0.0 24.9 %collective-permute-start = (bf16[8,512,128]{2,1,0:T(8,128)(2,1)}, bf16[8,512,128]{2,1,0:T(8,128)(2,1)S(1)}, u32[]{:S(2)}, u32[]{:S(2)}) collective-permute-start(bf16[8,512,128]{2,1,0:T(8,128)(2,1)} %own_ref.1), channel_id=1, source_target_pairs={{0,1},{1,0},{2,3},{3,2},{4,5},{5,4},{6,7},{7,6},{8,9},{9,8},{10,11... | collective-permute-start | bytes 3145736 | tf_op jit(solution)/shard_map/ppermute | solution.py:186
  3.9 20.9 %all-to-all-start = ((bf16[8,2,16,512]{3,2,1,0:T(8,128)(2,1)}), bf16[8,2,16,512]{3,2,1,0:T(8,128)(2,1)S(1)}, u32[]{:S(2)}, u32[]{:S(2)}) async-start(bf16[8,2,16,512]{3,2,1,0:T(8,128)(2,1)} %shard_map.100), calls=%async_computation | async-start | bytes 524288 | tf_op jit(solution)/shard_map/all_to_all | solution.py:23
  12.4 59.8 %collective-permute-start.2 = (bf16[448,2,1152]{2,1,0:T(2,128)(2,1)}, bf16[448,2,1152]{2,1,0:T(2,128)(2,1)}, u32[]{:S(2)}, u32[]{:S(2)}) collective-permute-start(bf16[448,2,1152]{2,1,0:T(2,128)(2,1)} %param.18), channel_id=1, source_target_pairs={{0,1},{1,0},{2,3},{3,2},{4,5},{5,4},{6,7},{7,6},{8,9},{9,8},{10,11... | collective-permute-start | bytes 6193160 | tf_op jit(solution)/shard_map/ppermute | solution.py:186
  26.5 7.6 %copy-start.6 = (bf16[1024,448]{0,1:T(8,128)(2,1)S(1)}, bf16[1024,448]{0,1:T(8,128)(2,1)}, u32[]{:S(2)}) copy-start(bf16[1024,448]{0,1:T(8,128)(2,1)} %param.16) | copy-start | bytes 2752516
  26.5 23.5 %all-to-all-start.1 = ((bf16[16,16,2048]{2,1,0:T(8,128)(2,1)}), bf16[16,16,2048]{2,1,0:T(8,128)(2,1)S(1)}, u32[]{:S(2)}, u32[]{:S(2)}) async-start(bf16[16,16,2048]{2,1,0:T(8,128)(2,1)} %bitcast.4), calls=%async_computation.1 | async-start | bytes 2097152 | tf_op jit(solution)/shard_map/all_to_all | solution.py:23
  34.1 21.1 %copy-start.7 = (bf16[448]{0:T(512)(128)(2,1)S(1)}, bf16[448]{0:T(512)(128)(2,1)}, u32[]{:S(2)}) copy-start(bf16[448]{0:T(512)(128)(2,1)} %param.17) | copy-start | bytes 2692
  34.1 2.6 %collective-permute-start.1 = (bf16[448,1024]{1,0:T(8,128)(2,1)S(1)}, bf16[448,1024]{1,0:T(8,128)(2,1)S(1)}, u32[]{:S(2)}, u32[]{:S(2)}) collective-permute-start(bf16[448,1024]{1,0:T(8,128)(2,1)S(1)} %bitcast.31), channel_id=1, source_target_pairs={{0,1},{1,0},{2,3},{3,2},{4,5},{5,4},{6,7},{7,6},{8,9},{9,8},{10,11... | collective-permute-start | bytes 2752520 | tf_op jit(solution)/shard_map/ppermute | solution.py:186
  51.4 14.5 %all-to-all-start.2 = ((bf16[16,16,448]{2,1,0:T(8,128)(2,1)}), bf16[16,16,448]{2,1,0:T(8,128)(2,1)S(1)}, u32[]{:S(2)}, u32[]{:S(2)}) async-start(bf16[16,16,448]{2,1,0:T(8,128)(2,1)} %bitcast.7), calls=%async_computation.2 | async-start | bytes 524288 | tf_op jit(solution)/shard_map/all_to_all | solution.py:23
  66.9 16.7 %all-to-all-start.3 = ((bf16[8,32,512]{2,1,0:T(8,128)(2,1)}), bf16[8,32,512]{2,1,0:T(8,128)(2,1)S(1)}, u32[]{:S(2)}, u32[]{:S(2)}) async-start(bf16[8,32,512]{2,1,0:T(8,128)(2,1)} %get-tuple-element.8), calls=%async_computation.3 | async-start | bytes 524288 | tf_op jit(solution)/shard_map/all_to_all | solution.py:23
  83.6 1.6 %copy-start.1 = (bf16[56,8,2,1152]{3,1,2,0:T(8,128)(2,1)S(1)}, bf16[56,8,2,1152]{3,1,2,0:T(8,128)(2,1)}, u32[]{:S(2)}) copy-start(bf16[56,8,2,1152]{3,1,2,0:T(8,128)(2,1)} %copy.14) | copy-start | bytes 6193156
  119.1 6.2 %copy-start.3 = (bf16[1152,448]{0,1:T(8,128)(2,1)S(1)}, bf16[1152,448]{0,1:T(8,128)(2,1)}, u32[]{:S(2)}) copy-start(bf16[1152,448]{0,1:T(8,128)(2,1)} %param.19) | copy-start | bytes 3096580
  120.4 21.4 %all-to-all-start.6 = ((bf16[16,16,2304]{2,1,0:T(8,128)(2,1)}), bf16[16,16,2304]{2,1,0:T(8,128)(2,1)S(1)}, u32[]{:S(2)}, u32[]{:S(2)}) async-start(bf16[16,16,2304]{2,1,0:T(8,128)(2,1)} %shard_map.106), calls=%async_computation.6 | async-start | bytes 2359296 | tf_op jit(solution)/shard_map/all_to_all | solution.py:23
  125.3 2.7 %collective-permute-start.3 = (bf16[448,1152]{1,0:T(8,128)(2,1)S(1)}, bf16[448,1152]{1,0:T(8,128)(2,1)S(1)}, u32[]{:S(2)}, u32[]{:S(2)}) collective-permute-start(bf16[448,1152]{1,0:T(8,128)(2,1)S(1)} %bitcast.29), channel_id=1, source_target_pairs={{0,1},{1,0},{2,3},{3,2},{4,5},{5,4},{6,7},{7,6},{8,9},{9,8},{10,11... | collective-permute-start | bytes 3096584 | tf_op jit(solution)/shard_map/ppermute | solution.py:186
  128.1 0.9 copy-start.4
  141.8 1.2 copy-start.5

commit v5 on v4

--- a/solution.py
+++ b/solution.py
@@ -25,7 +25,10 @@
     )
 
 
-def call(body, shapes, *args, smem=0, any_space=0, scratch=(), limit=8):
+def call(body, shapes, *args, smem=0, any_space=0, scratch=(), limit=8, flops=500000000):
+    arrays = jax.tree.leaves((args, shapes))
+    size = sum(a.size * a.dtype.itemsize for a in arrays)
+    cost = pl.CostEstimate(flops=flops, bytes_accessed=size, transcendentals=0)
     spaces = [pltpu.SMEM] * smem + [pltpu.HBM] * any_space
     spaces = spaces + [pltpu.VMEM] * (len(args) - len(spaces))
     return pl.pallas_call(
@@ -33,6 +36,7 @@
         out_shape=shapes,
         in_specs=[pl.BlockSpec(memory_space=space) for space in spaces],
         scratch_shapes=scratch,
+        cost_estimate=cost,
         compiler_params=pltpu.CompilerParams(vmem_limit_bytes=limit * 2**20),
     )(*args)
 
@@ -182,10 +186,8 @@
     core = lax.axis_index("c").reshape(1)
     out_proj = out_proj.T
     down_proj = down_proj.T
-    value_up, out_proj, gate_up, down_proj = [
-        (w, lax.ppermute(w, "c", [(0, 1), (1, 0)]))
-        for w in (value_up, out_proj, gate_up, down_proj)
-    ]
+    own = (value_up, out_proj, gate_up, down_proj)
+    other = [lax.ppermute(w, "c", [(0, 1), (1, 0)]) for w in own]
     attended = call(
         attend_body,
         shape((8, 2, 16, KL), BF),
@@ -204,6 +206,11 @@
         limit=60,
     )
     received = exchange(attended, "z").reshape(256, KL)
+    other[2] = other[2].reshape(other[2].shape[0], -1)
+    gate_up = gate_up.reshape(gate_up.shape[0], -1)
+    received, gate_up, other = lax.optimization_barrier((received, gate_up, other))
+    own = (value_up, out_proj, gate_up, down_proj)
+    value_up, out_proj, gate_up, down_proj = zip(own, other)
     values = call(value_body, shape((256, 2048), BF), core, received, *value_up, smem=1)
     values = exchange(values.reshape(16, 16, 2048), GRP).reshape(256, 2048)
     feats = residual.shape[1]
@@ -218,13 +225,13 @@
         norm_gain.reshape(1, feats),
     )
     packed = exchange(packed, "z").reshape(256, 512)
-    units = gate_up[0].shape[2]
+    units = gate_up[0].shape[1] // 2
     terms = call(
         units_body,
         shape((256, 4 * units + 128), BF),
         core,
         packed,
-        *[w.reshape(feats, 2 * units) for w in gate_up],
+        *gate_up,
         smem=1,
         scratch=[pltpu.VMEM((256, 512), BF)],
     )

time: 158 us -> 155 us (0.981)
  blocking collectives: 45 us -> 103 us
  waiting for transfers between devices: 62.5 us -> 17.8 us
  starting transfers between devices: 28.3 us -> 13 us
  local copies, waits for them, and re-layouts: 9.02 us -> 6.5 us
    all_to_all x3 -> x6, blocking collectives: 45 us -> 103 us  [exchange(): lax.all_to_all(parts, axes, split_axis=0, concat_axis=0, axis_index_group...]
    all_to_all x5 -> x2, waiting for transfers between devices: 57.4 us -> 17.8 us  [exchange(): lax.all_to_all(parts, axes, split_axis=0, concat_axis=0, axis_index_group...]
    all_to_all x5 -> x2, starting transfers between devices: 28 us -> 12 us  [exchange(): lax.all_to_all(parts, axes, split_axis=0, concat_axis=0, axis_index_group...]
    ppermute x4, waiting for transfers between devices: 5.09 us -> 0.01 us  [local(): other = [lax.ppermute(w, 'c', [(0, 1), (1, 0)]) for w in own]]
    unnamed x19 -> x15, local copies, waits for them, and re-layouts: 8.91 us -> 6.39 us
  transfers between devices with their start and end apart: 9 -> 6, of which waited for: 7 -> 2; matrix products, arithmetic and copies ran while one was open for 3% -> 3% of each run, Pallas kernels for 5% -> 2%
where the time goes in v5:
time: 155 us; the launch traced here: 154 us
  blocking collectives  103 us (66%)
  waiting for transfers between devices  17.8 us (11%)
  starting transfers between devices  13 us (8%)
  Pallas kernels  12 us (8%)
  local copies, waits for them, and re-layouts  6.5 us (4%)
    all_to_all x6, blocking collectives, exchange(): lax.all_to_all(parts, axes, split_axis=0, concat_axis=0, axis_index_group...  103 us
    all_to_all x2, waiting for transfers between devices, exchange(): lax.all_to_all(parts, axes, split_axis=0, concat_axis=0, axis_index_group...  17.8 us
    pallas_call x8, Pallas kernels, call(): pl.pallas_call(body, out_shape=shapes, in_specs=[pl.BlockSpec(memory_spac...  12 us
    all_to_all x2, starting transfers between devices, exchange(): lax.all_to_all(parts, axes, split_axis=0, concat_axis=0, axis_index_group...  12 us
    unnamed x15, local copies, waits for them, and re-layouts  6.39 us
  transfers between devices with their start and end apart: 6, of which 2 were waited for; matrix products, arithmetic and copies ran while one was open for 3% of the time, Pallas kernels for 2%

profile of v5, /device:TPU:2, one launch (start us, length us, event | category | flops | bytes accessed | tf_op | source)
XLA Modules:
  0.0 153.8 jit_solution(9414271799155896944)
XLA Ops:
  0.0 0.0 copy-start
  0.0 0.0 collective-permute-start.2
  0.0 0.5 collective-permute-start
  0.5 0.1 collective-permute-start.3
  0.6 0.4 collective-permute-start.1
  1.7 3.2 %shard_map.100 = bf16[8,2,16,512]{3,2,1,0:T(8,128)(2,1)} custom-call(s32[2]{0:T(128)} %len_hbm.1, s32[1]{0:T(128)S(6)} %copy.15.cnt_hbm, bf16[2,576,128]{2,1,0:T(8,128)(2,1)} %bitcast.36, bf16[2,576,512]{2,1,0:T(8,128)(2,1)} %bitcast.35), custom_call_target="tpu_custom_call" | custom-call | flops 500000000 | bytes 1736716 | tf_op jit(solution)/shard_map/pallas_call | solution.py:34
  4.8 8.5 %all-to-all-start = ((bf16[8,2,16,512]{3,2,1,0:T(8,128)(2,1)}), bf16[8,2,16,512]{3,2,1,0:T(8,128)(2,1)S(1)}, u32[]{:S(2)}, u32[]{:S(2)}) async-start(bf16[8,2,16,512]{3,2,1,0:T(8,128)(2,1)} %shard_map.100), calls=%async_computation | async-start | bytes 524288 | tf_op jit(solution)/shard_map/all_to_all | solution.py:23
  13.3 1.9 %copy.13 = bf16[56,8,2,1152]{3,1,2,0:T(8,128)(2,1)S(1)} copy(bf16[56,8,2,1152]{3,2,1,0:T(2,128)(2,1)} %bitcast.34) | data formatting | bytes 4128768
  15.2 0.0 collective-permute-done.2
  15.2 3.2 %copy.14 = bf16[56,8,2,1152]{3,1,2,0:T(8,128)(2,1)} copy(bf16[56,8,2,1152]{3,2,1,0:T(2,128)(2,1)} %bitcast.17) | data formatting | bytes 4128768
  18.4 7.0 %all-to-all-done = bf16[8,2,16,512]{3,2,1,0:T(8,128)(2,1)S(1)} async-done(((bf16[8,2,16,512]{3,2,1,0:T(8,128)(2,1)}), bf16[8,2,16,512]{3,2,1,0:T(8,128)(2,1)S(1)}, u32[]{:S(2)}, u32[]{:S(2)}) %all-to-all-start) | async-done | bytes 262176 | tf_op jit(solution)/shard_map/all_to_all | solution.py:23
  25.5 0.0 collective-permute-done.1.other_ref
  25.5 0.0 collective-permute-done.3.other_ref
  25.5 0.0 collective-permute-done.other_ref
  25.5 0.0 copy-start.2
  25.5 1.2 copy-done.2
  26.7 0.0 copy-start.4
  26.7 1.9 %shard_map.101 = bf16[256,2048]{1,0:T(8,128)(2,1)S(1)} custom-call(s32[1]{0:T(128)} %bitcast.core, bf16[256,512]{1,0:T(8,128)(2,1)S(1)} %bitcast.26, bf16[8,512,128]{2,1,0:T(8,128)(2,1)S(1)} %copy-done.2, bf16[8,512,128]{2,1,0:T(8,128)(2,1)} %collective-permute-done.other_ref), custom_call_target="tpu_custom_call" | custom-call | flops 500000000 | bytes 3407876 | tf_op jit(solution)/shard_map/pallas_call | solution.py:34
  28.6 22.2 %all_to_all.40 = bf16[16,16,2048]{2,1,0:T(8,128)(2,1)S(1)} all-to-all(bf16[16,16,2048]{2,1,0:T(8,128)(2,1)S(1)} %bitcast.24), channel_id=1, replica_groups=mesh['y'=4,'x'=4,'z'=8,'c'=2] {'y','x'}, dimensions={0} | all-to-all | bytes 2097152 | tf_op jit(solution)/shard_map/all_to_all | solution.py:23
  50.8 0.0 copy-start.5
  50.8 0.0 copy-done.4
  50.8 2.6 %shard_map.102 = bf16[256,448]{1,0:T(8,128)(2,1)} custom-call(bf16[256,2048]{1,0:T(8,128)(2,1)S(1)} %bitcast.23, bf16[448,1024]{1,0:T(8,128)(2,1)S(1)} %bitcast.32, bf16[448,1024]{1,0:T(8,128)(2,1)} %collective-permute-done.1.other_ref), custom_call_target="tpu_custom_call" | custom-call | flops 500000000 | bytes 3112960 | tf_op jit(solution)/shard_map/pallas_call | solution.py:34
  53.4 3.5 %all-to-all-start.2 = ((bf16[16,16,448]{2,1,0:T(8,128)(2,1)}), bf16[16,16,448]{2,1,0:T(8,128)(2,1)S(1)}, u32[]{:S(2)}, u32[]{:S(2)}) async-start(bf16[16,16,448]{2,1,0:T(8,128)(2,1)} %bitcast.8), calls=%async_computation.2 | async-start | bytes 524288 | tf_op jit(solution)/shard_map/all_to_all | solution.py:23
  56.9 0.0 copy-done
  57.0 0.1 constant_dynamic-slice_fusion
  57.1 0.1 copy.12.mine_ref
  57.2 0.0 copy-done.5
  57.2 10.8 %all-to-all-done.2 = bf16[16,16,448]{2,1,0:T(8,128)(2,1)S(1)} async-done(((bf16[16,16,448]{2,1,0:T(8,128)(2,1)}), bf16[16,16,448]{2,1,0:T(8,128)(2,1)S(1)}, u32[]{:S(2)}, u32[]{:S(2)}) %all-to-all-start.2) | async-done | bytes 229408 | tf_op jit(solution)/shard_map/all_to_all | solution.py:23
  67.9 0.0 copy-start.1
  67.9 0.3 shard_map.103
  68.2 16.0 %all_to_all.41 = bf16[8,32,512]{2,1,0:T(8,128)(2,1)S(1)} all-to-all(bf16[8,32,512]{2,1,0:T(8,128)(2,1)S(1)} %get-tuple-element.17), channel_id=1, replica_groups=mesh['y'=4,'x'=4,'z'=8,'c'=2] {'z'}, dimensions={0} | all-to-all | bytes 524288 | tf_op jit(solution)/shard_map/all_to_all | solution.py:23
  84.2 0.0 copy-done.1
  84.2 1.4 shard_map.104
  85.6 20.8 %all_to_all.42.p_ref = bf16[4,64,4736]{2,1,0:T(8,128)(2,1)S(1)} all-to-all(bf16[4,64,4736]{2,1,0:T(8,128)(2,1)S(1)} %bitcast.19), channel_id=1, replica_groups={{0,16,32,48},{64,80,96,112},{128,144,160,176},{192,208,224,240},{1,65,1..., dimensions={0} | all-to-all | bytes 4849664 | tf_op jit(solution)/shard_map/all_to_all | solution.py:23
  106.4 0.4 shard_map.105
  106.8 10.9 %all_to_all.43.p_ref = bf16[4,16,4736]{2,1,0:T(8,128)(2,1)S(1)} all-to-all(bf16[4,16,4736]{2,1,0:T(8,128)(2,1)S(1)} %bitcast.25), channel_id=1, replica_groups={{0,64,128,192},{16,80,144,208},{32,96,160,224},{48,112,176,240},{1,17,3..., dimensions={0} | all-to-all | bytes 1212416 | tf_op jit(solution)/shard_map/all_to_all | solution.py:23
  117.7 0.0 copy-start.3
  117.7 0.2 shard_map.106
  117.9 20.2 %all_to_all.44 = bf16[16,16,2304]{2,1,0:T(8,128)(2,1)S(1)} all-to-all(bf16[16,16,2304]{2,1,0:T(8,128)(2,1)S(1)} %shard_map.106), channel_id=1, replica_groups=mesh['y'=4,'x'=4,'z'=8,'c'=2] {'y','x'}, dimensions={0} | all-to-all | bytes 2359296 | tf_op jit(solution)/shard_map/all_to_all | solution.py:23
  138.2 0.0 copy-done.3
  138.2 2.1 %shard_map.107 = bf16[256,448]{1,0:T(8,128)(2,1)S(1)} custom-call(bf16[256,2304]{1,0:T(8,128)(2,1)S(1)} %bitcast.22, bf16[448,1152]{1,0:T(8,128)(2,1)S(1)} %bitcast.30, bf16[448,1152]{1,0:T(8,128)(2,1)} %collective-permute-done.3.other_ref), custom_call_target="tpu_custom_call" | custom-call | flops 500000000 | bytes 3473408 | tf_op jit(solution)/shard_map/pallas_call | solution.py:34
  140.2 12.9 %all_to_all.45 = bf16[8,32,448]{2,1,0:T(8,128)(2,1)S(1)} all-to-all(bf16[8,32,448]{2,1,0:T(8,128)(2,1)S(1)} %bitcast.28), channel_id=1, replica_groups=mesh['y'=4,'x'=4,'z'=8,'c'=2] {'z'}, dimensions={0} | all-to-all | bytes 458752 | tf_op jit(solution)/shard_map/all_to_all | solution.py:23
  153.2 0.6 add_convert_fusion
  (2 shorter events, 0.0 us)
Async XLA Ops:
  0.0 57.0 %copy-start = (bf16[512,448]{0,1:T(8,128)(2,1)S(1)}, bf16[512,448]{0,1:T(8,128)(2,1)}, u32[]{:S(2)}) copy-start(bf16[512,448]{0,1:T(8,128)(2,1)} %param.14) | copy-start | bytes 1376260
  0.0 15.2 %collective-permute-start.2 = (bf16[448,2,1152]{2,1,0:T(2,128)(2,1)}, bf16[448,2,1152]{2,1,0:T(2,128)(2,1)}, u32[]{:S(2)}, u32[]{:S(2)}) collective-permute-start(bf16[448,2,1152]{2,1,0:T(2,128)(2,1)} %param.18), channel_id=1, source_target_pairs={{0,1},{1,0},{2,3},{3,2},{4,5},{5,4},{6,7},{7,6},{8,9},{9,8},{10,11... | collective-permute-start | bytes 6193160 | tf_op jit(solution)/shard_map/ppermute | solution.py:190
  0.0 25.5 %collective-permute-start = (bf16[8,512,128]{2,1,0:T(8,128)(2,1)}, bf16[8,512,128]{2,1,0:T(8,128)(2,1)}, u32[]{:S(2)}, u32[]{:S(2)}) collective-permute-start(bf16[8,512,128]{2,1,0:T(8,128)(2,1)} %own_ref.1), channel_id=1, source_target_pairs={{0,1},{1,0},{2,3},{3,2},{4,5},{5,4},{6,7},{7,6},{8,9},{9,8},{10,11... | collective-permute-start | bytes 3145736 | tf_op jit(solution)/shard_map/ppermute | solution.py:190
  0.5 24.9 %collective-permute-start.3 = (bf16[448,1152]{1,0:T(8,128)(2,1)}, bf16[448,1152]{1,0:T(8,128)(2,1)}, u32[]{:S(2)}, u32[]{:S(2)}) collective-permute-start(bf16[448,1152]{1,0:T(8,128)(2,1)} %bitcast.29), channel_id=1, source_target_pairs={{0,1},{1,0},{2,3},{3,2},{4,5},{5,4},{6,7},{7,6},{8,9},{9,8},{10,11... | collective-permute-start | bytes 3096584 | tf_op jit(solution)/shard_map/ppermute | solution.py:190
  0.6 24.8 %collective-permute-start.1 = (bf16[448,1024]{1,0:T(8,128)(2,1)}, bf16[448,1024]{1,0:T(8,128)(2,1)}, u32[]{:S(2)}, u32[]{:S(2)}) collective-permute-start(bf16[448,1024]{1,0:T(8,128)(2,1)} %bitcast.31), channel_id=1, source_target_pairs={{0,1},{1,0},{2,3},{3,2},{4,5},{5,4},{6,7},{7,6},{8,9},{9,8},{10,11... | collective-permute-start | bytes 2752520 | tf_op jit(solution)/shard_map/ppermute | solution.py:190
  4.8 20.6 %all-to-all-start = ((bf16[8,2,16,512]{3,2,1,0:T(8,128)(2,1)}), bf16[8,2,16,512]{3,2,1,0:T(8,128)(2,1)S(1)}, u32[]{:S(2)}, u32[]{:S(2)}) async-start(bf16[8,2,16,512]{3,2,1,0:T(8,128)(2,1)} %shard_map.100), calls=%async_computation | async-start | bytes 524288 | tf_op jit(solution)/shard_map/all_to_all | solution.py:23
  25.5 1.2 copy-start.2
  26.7 24.1 %copy-start.4 = (bf16[1024,448]{0,1:T(8,128)(2,1)S(1)}, bf16[1024,448]{0,1:T(8,128)(2,1)}, u32[]{:S(2)}) copy-start(bf16[1024,448]{0,1:T(8,128)(2,1)} %param.16) | copy-start | bytes 2752516
  50.8 6.4 %copy-start.5 = (bf16[448]{0:T(512)(128)(2,1)S(1)}, bf16[448]{0:T(512)(128)(2,1)}, u32[]{:S(2)}) copy-start(bf16[448]{0:T(512)(128)(2,1)} %param.17) | copy-start | bytes 2692
  53.4 14.5 %all-to-all-start.2 = ((bf16[16,16,448]{2,1,0:T(8,128)(2,1)}), bf16[16,16,448]{2,1,0:T(8,128)(2,1)S(1)}, u32[]{:S(2)}, u32[]{:S(2)}) async-start(bf16[16,16,448]{2,1,0:T(8,128)(2,1)} %bitcast.8), calls=%async_computation.2 | async-start | bytes 524288 | tf_op jit(solution)/shard_map/all_to_all | solution.py:23
  67.9 16.3 %copy-start.1 = (bf16[56,8,2,1152]{3,1,2,0:T(8,128)(2,1)S(1)}, bf16[56,8,2,1152]{3,1,2,0:T(8,128)(2,1)}, u32[]{:S(2)}) copy-start(bf16[56,8,2,1152]{3,1,2,0:T(8,128)(2,1)} %copy.14) | copy-start | bytes 6193156
  117.7 20.5 %copy-start.3 = (bf16[1152,448]{0,1:T(8,128)(2,1)S(1)}, bf16[1152,448]{0,1:T(8,128)(2,1)}, u32[]{:S(2)}) copy-start(bf16[1152,448]{0,1:T(8,128)(2,1)} %param.19) | copy-start | bytes 3096580

commit v6 on v5

--- a/solution.py
+++ b/solution.py
@@ -29,6 +29,7 @@
     arrays = jax.tree.leaves((args, shapes))
     size = sum(a.size * a.dtype.itemsize for a in arrays)
     cost = pl.CostEstimate(flops=flops, bytes_accessed=size, transcendentals=0)
+    cost = cost if flops else None
     spaces = [pltpu.SMEM] * smem + [pltpu.HBM] * any_space
     spaces = spaces + [pltpu.VMEM] * (len(args) - len(spaces))
     return pl.pallas_call(
@@ -168,6 +169,10 @@
             at = i * units + j
             for r in range(16):
                 o_ref[r, :, at : at + step] = hidden
+
+
+def last_body(c_ref, p_ref, o_ref):
+    o_ref[...] = (c_ref[...] + jnp.sum(p_ref[...].astype(F32), axis=0)).astype(BF)
 
 
 def local(
@@ -208,21 +213,32 @@
     received = exchange(attended, "z").reshape(256, KL)
     other[2] = other[2].reshape(other[2].shape[0], -1)
     gate_up = gate_up.reshape(gate_up.shape[0], -1)
-    received, gate_up, other = lax.optimization_barrier((received, gate_up, other))
+    mine = lax.dynamic_slice_in_dim(residual, lax.axis_index(TP) * 32, 32, 0)
+    gain = norm_gain.reshape(1, -1)
+    received, gate_up, other, mine, gain = lax.optimization_barrier(
+        (received, gate_up, other, mine, gain)
+    )
     own = (value_up, out_proj, gate_up, down_proj)
     value_up, out_proj, gate_up, down_proj = zip(own, other)
-    values = call(value_body, shape((256, 2048), BF), core, received, *value_up, smem=1)
+    values = call(
+        value_body,
+        shape((256, 2048), BF),
+        core,
+        received,
+        *value_up,
+        smem=1,
+        flops=0,
+    )
     values = exchange(values.reshape(16, 16, 2048), GRP).reshape(256, 2048)
     feats = residual.shape[1]
     partial = call(out_body, shape((256, feats), BF), values, *out_proj)
     pieces = exchange(partial.reshape(16, 16, feats), TP).reshape(256, feats)
-    mine = lax.dynamic_slice_in_dim(residual, lax.axis_index(TP) * 32, 32, 0)
     combined, packed = call(
         mix_body,
         (shape((32, feats), F32), shape((8, 32, 512), BF)),
         pieces,
         mine,
-        norm_gain.reshape(1, feats),
+        gain,
     )
     packed = exchange(packed, "z").reshape(256, 512)
     units = gate_up[0].shape[1] // 2
@@ -242,7 +258,7 @@
     hidden = exchange(hidden, GRP).reshape(256, 2 * units)
     last = call(out_body, shape((256, feats), BF), hidden, *down_proj)
     last = exchange(last.reshape(8, 32, feats), "z")
-    return (combined + jnp.sum(last.astype(F32), axis=0)).astype(BF)
+    return call(last_body, shape((32, feats), BF), combined, last)
 
 
 def solution(mesh):

time: 155 us -> 153 us (0.987)
  blocking collectives: 103 us -> 117 us
  waiting for transfers between devices: 17.8 us -> 6.84 us
  starting transfers between devices: 13 us -> 9.49 us
    all_to_all x6 -> x7, blocking collectives: 103 us -> 117 us  [exchange(): lax.all_to_all(parts, axes, split_axis=0, concat_axis=0, axis_index_group...]
    all_to_all x2 -> x1, waiting for transfers between devices: 17.8 us -> 6.83 us  [exchange(): lax.all_to_all(parts, axes, split_axis=0, concat_axis=0, axis_index_group...]
    all_to_all x2 -> x1, starting transfers between devices: 12 us -> 8.48 us  [exchange(): lax.all_to_all(parts, axes, split_axis=0, concat_axis=0, axis_index_group...]
    unnamed x15 -> x14, local copies, waits for them, and re-layouts: 6.39 us -> 6.3 us
    pallas_call x8 -> x9, Pallas kernels: 12 us -> 12 us  [call(): pl.pallas_call(body, out_shape=shapes, in_specs=[pl.BlockSpec(memory_spac...]
  transfers between devices with their start and end apart: 6 -> 5, of which waited for: 2 -> 1; matrix products, arithmetic and copies ran while one was open for 3% -> 3% of each run, Pallas kernels for 2% -> 2%
where the time goes in v6:
time: 153 us; the launch traced here: 152 us
  blocking collectives  117 us (76%)
  Pallas kernels  12 us (8%)
  starting transfers between devices  9.49 us (6%)
  waiting for transfers between devices  6.84 us (4%)
  local copies, waits for them, and re-layouts  6.48 us (4%)
    all_to_all x7, blocking collectives, exchange(): lax.all_to_all(parts, axes, split_axis=0, concat_axis=0, axis_index_group...  117 us
    pallas_call x9, Pallas kernels, call(): pl.pallas_call(body, out_shape=shapes, in_specs=[pl.BlockSpec(memory_spac...  12 us
    all_to_all x1, starting transfers between devices, exchange(): lax.all_to_all(parts, axes, split_axis=0, concat_axis=0, axis_index_group...  8.48 us
    all_to_all x1, waiting for transfers between devices, exchange(): lax.all_to_all(parts, axes, split_axis=0, concat_axis=0, axis_index_group...  6.83 us
    unnamed x14, local copies, waits for them, and re-layouts  6.3 us
  transfers between devices with their start and end apart: 5, of which 1 were waited for; matrix products, arithmetic and copies ran while one was open for 3% of the time, Pallas kernels for 2%

profile of v6, /device:TPU:2, one launch (start us, length us, event | category | flops | bytes accessed | tf_op | source)
XLA Modules:
  0.0 152.2 jit_solution(7776625400151937064)
XLA Ops:
  0.0 0.0 copy-start
  0.0 0.0 collective-permute-start.2
  0.0 0.5 collective-permute-start
  0.5 0.1 collective-permute-start.3
  0.6 0.4 collective-permute-start.1
  1.7 3.2 %shard_map.100 = bf16[8,2,16,512]{3,2,1,0:T(8,128)(2,1)} custom-call(s32[2]{0:T(128)} %len_hbm.1, s32[1]{0:T(128)S(6)} %copy.15.cnt_hbm, bf16[2,576,128]{2,1,0:T(8,128)(2,1)} %bitcast.37, bf16[2,576,512]{2,1,0:T(8,128)(2,1)} %bitcast.36), custom_call_target="tpu_custom_call" | custom-call | flops 500000000 | bytes 1736716 | tf_op jit(solution)/shard_map/pallas_call | solution.py:35
  4.8 8.5 %all-to-all-start = ((bf16[8,2,16,512]{3,2,1,0:T(8,128)(2,1)}), bf16[8,2,16,512]{3,2,1,0:T(8,128)(2,1)S(1)}, u32[]{:S(2)}, u32[]{:S(2)}) async-start(bf16[8,2,16,512]{3,2,1,0:T(8,128)(2,1)} %shard_map.100), calls=%async_computation | async-start | bytes 524288 | tf_op jit(solution)/shard_map/all_to_all | solution.py:23
  13.3 0.0 copy-done
  13.3 0.1 constant_dynamic-slice_fusion
  13.4 0.1 copy.12.mine_ref
  13.5 0.0 copy-start.5
  13.5 1.9 %copy.13 = bf16[56,8,2,1152]{3,1,2,0:T(8,128)(2,1)S(1)} copy(bf16[56,8,2,1152]{3,2,1,0:T(2,128)(2,1)} %bitcast.35) | data formatting | bytes 4128768
  15.4 0.0 copy-done.5
  15.4 0.0 collective-permute-done.2
  15.4 3.2 %copy.14 = bf16[56,8,2,1152]{3,1,2,0:T(8,128)(2,1)} copy(bf16[56,8,2,1152]{3,2,1,0:T(2,128)(2,1)} %bitcast.17) | data formatting | bytes 4128768
  18.6 6.8 %all-to-all-done = bf16[8,2,16,512]{3,2,1,0:T(8,128)(2,1)S(1)} async-done(((bf16[8,2,16,512]{3,2,1,0:T(8,128)(2,1)}), bf16[8,2,16,512]{3,2,1,0:T(8,128)(2,1)S(1)}, u32[]{:S(2)}, u32[]{:S(2)}) %all-to-all-start) | async-done | bytes 262176 | tf_op jit(solution)/shard_map/all_to_all | solution.py:23
  25.5 0.0 collective-permute-done.1.other_ref
  25.5 0.0 collective-permute-done.3.other_ref
  25.5 0.0 collective-permute-done.other_ref
  25.5 0.0 copy-start.2
  25.5 1.2 copy-done.2
  26.7 0.0 copy-start.4
  26.7 1.9 %shard_map.101 = bf16[256,2048]{1,0:T(8,128)(2,1)S(1)} custom-call(s32[1]{0:T(128)} %bitcast.core, bf16[256,512]{1,0:T(8,128)(2,1)S(1)} %bitcast.26, bf16[8,512,128]{2,1,0:T(8,128)(2,1)S(1)} %copy-done.2, bf16[8,512,128]{2,1,0:T(8,128)(2,1)} %collective-permute-done.other_ref), custom_call_target="tpu_custom_call" | custom-call | tf_op jit(solution)/shard_map/pallas_call | solution.py:35
  28.6 22.2 %all_to_all.40 = bf16[16,16,2048]{2,1,0:T(8,128)(2,1)S(1)} all-to-all(bf16[16,16,2048]{2,1,0:T(8,128)(2,1)S(1)} %bitcast.24), channel_id=1, replica_groups=mesh['y'=4,'x'=4,'z'=8,'c'=2] {'y','x'}, dimensions={0} | all-to-all | bytes 2097152 | tf_op jit(solution)/shard_map/all_to_all | solution.py:23
  50.8 0.0 copy-done.4
  50.8 1.9 %shard_map.102 = bf16[256,448]{1,0:T(8,128)(2,1)S(1)} custom-call(bf16[256,2048]{1,0:T(8,128)(2,1)S(1)} %bitcast.23, bf16[448,1024]{1,0:T(8,128)(2,1)S(1)} %bitcast.33, bf16[448,1024]{1,0:T(8,128)(2,1)} %collective-permute-done.1.other_ref), custom_call_target="tpu_custom_call" | custom-call | flops 500000000 | bytes 3112960 | tf_op jit(solution)/shard_map/pallas_call | solution.py:35
  52.7 0.0 copy-start.1
  52.7 13.8 %all_to_all.41 = bf16[16,16,448]{2,1,0:T(8,128)(2,1)S(1)} all-to-all(bf16[16,16,448]{2,1,0:T(8,128)(2,1)S(1)} %bitcast.28), channel_id=1, replica_groups=mesh['y'=4,'x'=4,'z'=8,'c'=2] {'z','c'}, dimensions={0} | all-to-all | bytes 458752 | tf_op jit(solution)/shard_map/all_to_all | solution.py:23
  66.5 0.3 shard_map.103
  66.7 15.9 %all_to_all.42 = bf16[8,32,512]{2,1,0:T(8,128)(2,1)S(1)} all-to-all(bf16[8,32,512]{2,1,0:T(8,128)(2,1)S(1)} %get-tuple-element.21), channel_id=1, replica_groups=mesh['y'=4,'x'=4,'z'=8,'c'=2] {'z'}, dimensions={0} | all-to-all | bytes 524288 | tf_op jit(solution)/shard_map/all_to_all | solution.py:23
  82.6 0.0 copy-done.1
  82.6 1.4 shard_map.104
  84.0 20.8 %all_to_all.43.p_ref = bf16[4,64,4736]{2,1,0:T(8,128)(2,1)S(1)} all-to-all(bf16[4,64,4736]{2,1,0:T(8,128)(2,1)S(1)} %bitcast.19), channel_id=1, replica_groups={{0,16,32,48},{64,80,96,112},{128,144,160,176},{192,208,224,240},{1,65,1..., dimensions={0} | all-to-all | bytes 4849664 | tf_op jit(solution)/shard_map/all_to_all | solution.py:23
  104.8 0.4 shard_map.105
  105.2 10.9 %all_to_all.44.p_ref = bf16[4,16,4736]{2,1,0:T(8,128)(2,1)S(1)} all-to-all(bf16[4,16,4736]{2,1,0:T(8,128)(2,1)S(1)} %bitcast.25), channel_id=1, replica_groups={{0,64,128,192},{16,80,144,208},{32,96,160,224},{48,112,176,240},{1,17,3..., dimensions={0} | all-to-all | bytes 1212416 | tf_op jit(solution)/shard_map/all_to_all | solution.py:23
  116.1 0.0 copy-start.3
  116.1 0.2 shard_map.106
  116.3 20.2 %all_to_all.45 = bf16[16,16,2304]{2,1,0:T(8,128)(2,1)S(1)} all-to-all(bf16[16,16,2304]{2,1,0:T(8,128)(2,1)S(1)} %shard_map.106), channel_id=1, replica_groups=mesh['y'=4,'x'=4,'z'=8,'c'=2] {'y','x'}, dimensions={0} | all-to-all | bytes 2359296 | tf_op jit(solution)/shard_map/all_to_all | solution.py:23
  136.5 0.0 copy-done.3
  136.6 2.1 %shard_map.107 = bf16[256,448]{1,0:T(8,128)(2,1)S(1)} custom-call(bf16[256,2304]{1,0:T(8,128)(2,1)S(1)} %bitcast.22, bf16[448,1152]{1,0:T(8,128)(2,1)S(1)} %bitcast.31, bf16[448,1152]{1,0:T(8,128)(2,1)} %collective-permute-done.3.other_ref), custom_call_target="tpu_custom_call" | custom-call | flops 500000000 | bytes 3473408 | tf_op jit(solution)/shard_map/pallas_call | solution.py:35
  138.6 12.9 %all_to_all.46.p_ref = bf16[8,32,448]{2,1,0:T(8,128)(2,1)S(1)} all-to-all(bf16[8,32,448]{2,1,0:T(8,128)(2,1)S(1)} %bitcast.29), channel_id=1, replica_groups=mesh['y'=4,'x'=4,'z'=8,'c'=2] {'z'}, dimensions={0} | all-to-all | bytes 458752 | tf_op jit(solution)/shard_map/all_to_all | solution.py:23
  151.5 0.7 shard_map.108
  (1 shorter events, 0.0 us)
Async XLA Ops:
  0.0 13.3 %copy-start = (bf16[512,448]{0,1:T(8,128)(2,1)S(1)}, bf16[512,448]{0,1:T(8,128)(2,1)}, u32[]{:S(2)}) copy-start(bf16[512,448]{0,1:T(8,128)(2,1)} %param.14) | copy-start | bytes 1376260
  0.0 15.4 %collective-permute-start.2 = (bf16[448,2,1152]{2,1,0:T(2,128)(2,1)}, bf16[448,2,1152]{2,1,0:T(2,128)(2,1)}, u32[]{:S(2)}, u32[]{:S(2)}) collective-permute-start(bf16[448,2,1152]{2,1,0:T(2,128)(2,1)} %param.18), channel_id=1, source_target_pairs={{0,1},{1,0},{2,3},{3,2},{4,5},{5,4},{6,7},{7,6},{8,9},{9,8},{10,11... | collective-permute-start | bytes 6193160 | tf_op jit(solution)/shard_map/ppermute | solution.py:195
  0.0 25.5 %collective-permute-start = (bf16[8,512,128]{2,1,0:T(8,128)(2,1)}, bf16[8,512,128]{2,1,0:T(8,128)(2,1)}, u32[]{:S(2)}, u32[]{:S(2)}) collective-permute-start(bf16[8,512,128]{2,1,0:T(8,128)(2,1)} %own_ref.1), channel_id=1, source_target_pairs={{0,1},{1,0},{2,3},{3,2},{4,5},{5,4},{6,7},{7,6},{8,9},{9,8},{10,11... | collective-permute-start | bytes 3145736 | tf_op jit(solution)/shard_map/ppermute | solution.py:195
  0.5 24.9 %collective-permute-start.3 = (bf16[448,1152]{1,0:T(8,128)(2,1)}, bf16[448,1152]{1,0:T(8,128)(2,1)}, u32[]{:S(2)}, u32[]{:S(2)}) collective-permute-start(bf16[448,1152]{1,0:T(8,128)(2,1)} %bitcast.30), channel_id=1, source_target_pairs={{0,1},{1,0},{2,3},{3,2},{4,5},{5,4},{6,7},{7,6},{8,9},{9,8},{10,11... | collective-permute-start | bytes 3096584 | tf_op jit(solution)/shard_map/ppermute | solution.py:195
  0.6 24.8 %collective-permute-start.1 = (bf16[448,1024]{1,0:T(8,128)(2,1)}, bf16[448,1024]{1,0:T(8,128)(2,1)}, u32[]{:S(2)}, u32[]{:S(2)}) collective-permute-start(bf16[448,1024]{1,0:T(8,128)(2,1)} %bitcast.32), channel_id=1, source_target_pairs={{0,1},{1,0},{2,3},{3,2},{4,5},{5,4},{6,7},{7,6},{8,9},{9,8},{10,11... | collective-permute-start | bytes 2752520 | tf_op jit(solution)/shard_map/ppermute | solution.py:195
  4.8 20.6 %all-to-all-start = ((bf16[8,2,16,512]{3,2,1,0:T(8,128)(2,1)}), bf16[8,2,16,512]{3,2,1,0:T(8,128)(2,1)S(1)}, u32[]{:S(2)}, u32[]{:S(2)}) async-start(bf16[8,2,16,512]{3,2,1,0:T(8,128)(2,1)} %shard_map.100), calls=%async_computation | async-start | bytes 524288 | tf_op jit(solution)/shard_map/all_to_all | solution.py:23
  13.5 1.9 %copy-start.5 = (bf16[448]{0:T(512)(128)(2,1)S(1)}, bf16[448]{0:T(512)(128)(2,1)}, u32[]{:S(2)}) copy-start(bf16[448]{0:T(512)(128)(2,1)} %param.17) | copy-start | bytes 2692
  25.5 1.2 copy-start.2
  26.7 24.1 %copy-start.4 = (bf16[1024,448]{0,1:T(8,128)(2,1)S(1)}, bf16[1024,448]{0,1:T(8,128)(2,1)}, u32[]{:S(2)}) copy-start(bf16[1024,448]{0,1:T(8,128)(2,1)} %param.16) | copy-start | bytes 2752516
  52.7 29.9 %copy-start.1 = (bf16[56,8,2,1152]{3,1,2,0:T(8,128)(2,1)S(1)}, bf16[56,8,2,1152]{3,1,2,0:T(8,128)(2,1)}, u32[]{:S(2)}) copy-start(bf16[56,8,2,1152]{3,1,2,0:T(8,128)(2,1)} %copy.14) | copy-start | bytes 6193156
  116.1 20.5 %copy-start.3 = (bf16[1152,448]{0,1:T(8,128)(2,1)S(1)}, bf16[1152,448]{0,1:T(8,128)(2,1)}, u32[]{:S(2)}) copy-start(bf16[1152,448]{0,1:T(8,128)(2,1)} %param.19) | copy-start | bytes 3096580

commit v7 on v6

--- a/solution.py
+++ b/solution.py
@@ -211,6 +211,8 @@
         limit=60,
     )
     received = exchange(attended, "z").reshape(256, KL)
+    one = (core[0] < 2).astype(BF)
+    other = [other[0], other[1] * one, other[2], other[3] * one]
     other[2] = other[2].reshape(other[2].shape[0], -1)
     gate_up = gate_up.reshape(gate_up.shape[0], -1)
     mine = lax.dynamic_slice_in_dim(residual, lax.axis_index(TP) * 32, 32, 0)

time: 153 us -> 152 us (level)
  waiting for transfers between devices: 6.84 us -> 3.41 us
  other arithmetic: 0 us -> 2.34 us
  Pallas kernels: 12 us -> 9.74 us
    all_to_all x1, waiting for transfers between devices: 6.83 us -> 3.4 us  [exchange(): lax.all_to_all(parts, axes, split_axis=0, concat_axis=0, axis_index_group...]
    mul x0 -> x2, other arithmetic: none -> 2.34 us  [local(): other = [other[0], other[1] * one, other[2], other[3] * one]]
    pallas_call x9, Pallas kernels: 12 us -> 9.74 us  [call(): pl.pallas_call(body, out_shape=shapes, in_specs=[pl.BlockSpec(memory_spac...]
    all_to_all x7, blocking collectives: 117 us -> 118 us  [exchange(): lax.all_to_all(parts, axes, split_axis=0, concat_axis=0, axis_index_group...]
    unnamed x14 -> x20, local copies, waits for them, and re-layouts: 6.3 us -> 6.33 us
  transfers between devices with their start and end apart: 5 -> 5, of which waited for: 1 -> 1; matrix products, arithmetic and copies ran while one was open for 3% -> 6% of each run, Pallas kernels for 2% -> 2%
where the time goes in v7:
time: 152 us
  blocking collectives  118 us (78%)
  Pallas kernels  9.74 us (6%)
  starting transfers between devices  9.49 us (6%)
  local copies, waits for them, and re-layouts  7.71 us (5%)
  waiting for transfers between devices  3.41 us (2%)
  other arithmetic  2.34 us (2%)
    all_to_all x7, blocking collectives, exchange(): lax.all_to_all(parts, axes, split_axis=0, concat_axis=0, axis_index_group...  118 us
    pallas_call x9, Pallas kernels, call(): pl.pallas_call(body, out_shape=shapes, in_specs=[pl.BlockSpec(memory_spac...  9.74 us
    all_to_all x1, starting transfers between devices, exchange(): lax.all_to_all(parts, axes, split_axis=0, concat_axis=0, axis_index_group...  8.48 us
    unnamed x20, local copies, waits for them, and re-layouts  6.33 us
    all_to_all x1, waiting for transfers between devices, exchange(): lax.all_to_all(parts, axes, split_axis=0, concat_axis=0, axis_index_group...  3.4 us
  transfers between devices with their start and end apart: 5, of which 1 were waited for; matrix products, arithmetic and copies ran while one was open for 6% of the time, Pallas kernels for 2%

profile of v7, /device:TPU:2, one launch (start us, length us, event | category | flops | bytes accessed | tf_op | source)
XLA Modules:
  0.0 151.7 jit_solution(15413351819111949145)
XLA Ops:
  0.0 0.0 copy-start
  0.0 0.0 collective-permute-start.2
  0.0 0.5 collective-permute-start.1
  0.5 0.1 collective-permute-start.3
  0.6 0.4 collective-permute-start
  1.7 3.2 %shard_map.100 = bf16[8,2,16,512]{3,2,1,0:T(8,128)(2,1)} custom-call(s32[2]{0:T(128)} %len_hbm.1, s32[1]{0:T(128)S(6)} %copy.15.cnt_hbm, bf16[2,576,128]{2,1,0:T(8,128)(2,1)} %bitcast.36, bf16[2,576,512]{2,1,0:T(8,128)(2,1)} %bitcast.35), custom_call_target="tpu_custom_call" | custom-call | flops 500000000 | bytes 1736716 | tf_op jit(solution)/shard_map/pallas_call | solution.py:35
  4.8 8.5 %all-to-all-start = ((bf16[8,2,16,512]{3,2,1,0:T(8,128)(2,1)}), bf16[8,2,16,512]{3,2,1,0:T(8,128)(2,1)}, u32[]{:S(2)}, u32[]{:S(2)}) async-start(bf16[8,2,16,512]{3,2,1,0:T(8,128)(2,1)} %shard_map.100), calls=%async_computation | async-start | bytes 524288 | tf_op jit(solution)/shard_map/all_to_all | solution.py:23
  13.3 0.0 copy-done
  13.3 0.1 constant_dynamic-slice_fusion
  13.4 0.7 copy.12.mine_ref
  14.1 0.0 copy-start.8
  14.1 1.9 %copy.13 = bf16[56,8,2,1152]{3,1,2,0:T(8,128)(2,1)S(1)} copy(bf16[56,8,2,1152]{3,2,1,0:T(2,128)(2,1)} %bitcast.34) | data formatting | bytes 4128768
  16.0 0.0 copy-done.8
  16.0 0.6 reshape.46.gain_ref
  16.6 0.0 collective-permute-done.1
  16.6 1.0 broadcast_multiply_fusion.1.other_ref
  17.6 0.0 collective-permute-done.3
  17.6 1.3 broadcast_multiply_fusion.other_ref
  19.0 0.0 collective-permute-done.2
  19.0 3.2 %copy.14 = bf16[56,8,2,1152]{3,1,2,0:T(8,128)(2,1)} copy(bf16[56,8,2,1152]{3,2,1,0:T(2,128)(2,1)} %bitcast.17) | data formatting | bytes 4128768
  22.2 3.4 %all-to-all-done = bf16[8,2,16,512]{3,2,1,0:T(8,128)(2,1)} async-done(((bf16[8,2,16,512]{3,2,1,0:T(8,128)(2,1)}), bf16[8,2,16,512]{3,2,1,0:T(8,128)(2,1)}, u32[]{:S(2)}, u32[]{:S(2)}) %all-to-all-start) | async-done | bytes 262176 | tf_op jit(solution)/shard_map/all_to_all | solution.py:23
  25.6 0.0 collective-permute-done.other_ref
  25.6 0.0 copy-start.3
  25.6 1.2 copy-done.3
  26.8 0.0 copy-start.2
  26.8 0.0 copy-start.5
  26.8 2.1 %shard_map.101 = bf16[256,2048]{1,0:T(8,128)(2,1)S(1)} custom-call(s32[1]{0:T(128)} %bitcast.core, bf16[256,512]{1,0:T(8,128)(2,1)} %bitcast.3.x_ref, bf16[8,512,128]{2,1,0:T(8,128)(2,1)S(1)} %copy-done.3, bf16[8,512,128]{2,1,0:T(8,128)(2,1)} %collective-permute-done.other_ref), custom_call_target="tpu_custom_call" | custom-call | tf_op jit(solution)/shard_map/pallas_call | solution.py:35
  28.9 22.2 %all_to_all.40 = bf16[16,16,2048]{2,1,0:T(8,128)(2,1)S(1)} all-to-all(bf16[16,16,2048]{2,1,0:T(8,128)(2,1)S(1)} %bitcast.24), channel_id=1, replica_groups=mesh['y'=4,'x'=4,'z'=8,'c'=2] {'y','x'}, dimensions={0} | all-to-all | bytes 2097152 | tf_op jit(solution)/shard_map/all_to_all | solution.py:23
  51.0 0.0 copy-start.6
  51.0 0.0 copy-start.7
  51.0 0.0 copy-done.2
  51.0 0.0 copy-done.5
  51.0 0.7 shard_map.102
  51.8 0.0 copy-start.1
  51.8 15.6 %all_to_all.41 = bf16[16,16,448]{2,1,0:T(8,128)(2,1)S(1)} all-to-all(bf16[16,16,448]{2,1,0:T(8,128)(2,1)S(1)} %bitcast.27), channel_id=1, replica_groups=mesh['y'=4,'x'=4,'z'=8,'c'=2] {'z','c'}, dimensions={0} | all-to-all | bytes 458752 | tf_op jit(solution)/shard_map/all_to_all | solution.py:23
  67.4 0.0 copy-done.6
  67.4 0.0 copy-done.7
  67.4 0.3 shard_map.103
  67.7 15.7 %all_to_all.42 = bf16[8,32,512]{2,1,0:T(8,128)(2,1)S(1)} all-to-all(bf16[8,32,512]{2,1,0:T(8,128)(2,1)S(1)} %get-tuple-element.21), channel_id=1, replica_groups=mesh['y'=4,'x'=4,'z'=8,'c'=2] {'z'}, dimensions={0} | all-to-all | bytes 524288 | tf_op jit(solution)/shard_map/all_to_all | solution.py:23
  83.3 0.0 copy-done.1
  83.3 1.4 shard_map.104
  84.8 20.7 %all_to_all.43.p_ref = bf16[4,64,4736]{2,1,0:T(8,128)(2,1)S(1)} all-to-all(bf16[4,64,4736]{2,1,0:T(8,128)(2,1)S(1)} %bitcast.19), channel_id=1, replica_groups={{0,16,32,48},{64,80,96,112},{128,144,160,176},{192,208,224,240},{1,65,1..., dimensions={0} | all-to-all | bytes 4849664 | tf_op jit(solution)/shard_map/all_to_all | solution.py:23
  105.5 0.4 shard_map.105
  105.9 10.9 %all_to_all.44.p_ref = bf16[4,16,4736]{2,1,0:T(8,128)(2,1)S(1)} all-to-all(bf16[4,16,4736]{2,1,0:T(8,128)(2,1)S(1)} %bitcast.25), channel_id=1, replica_groups={{0,64,128,192},{16,80,144,208},{32,96,160,224},{48,112,176,240},{1,17,3..., dimensions={0} | all-to-all | bytes 1212416 | tf_op jit(solution)/shard_map/all_to_all | solution.py:23
  116.8 0.0 copy-start.4
  116.8 0.2 shard_map.106
  117.0 20.2 %all_to_all.45 = bf16[16,16,2304]{2,1,0:T(8,128)(2,1)S(1)} all-to-all(bf16[16,16,2304]{2,1,0:T(8,128)(2,1)S(1)} %shard_map.106), channel_id=1, replica_groups=mesh['y'=4,'x'=4,'z'=8,'c'=2] {'y','x'}, dimensions={0} | all-to-all | bytes 2359296 | tf_op jit(solution)/shard_map/all_to_all | solution.py:23
  137.3 0.0 copy-done.4
  137.3 0.9 shard_map.107
  138.1 12.9 %all_to_all.46.p_ref = bf16[8,32,448]{2,1,0:T(8,128)(2,1)S(1)} all-to-all(bf16[8,32,448]{2,1,0:T(8,128)(2,1)S(1)} %bitcast.28), channel_id=1, replica_groups=mesh['y'=4,'x'=4,'z'=8,'c'=2] {'z'}, dimensions={0} | all-to-all | bytes 458752 | tf_op jit(solution)/shard_map/all_to_all | solution.py:23
  151.0 0.7 shard_map.108
Async XLA Ops:
  0.0 13.3 %copy-start = (bf16[512,448]{0,1:T(8,128)(2,1)S(1)}, bf16[512,448]{0,1:T(8,128)(2,1)}, u32[]{:S(2)}) copy-start(bf16[512,448]{0,1:T(8,128)(2,1)} %param.14) | copy-start | bytes 1376260
  0.0 19.0 %collective-permute-start.2 = (bf16[448,2,1152]{2,1,0:T(2,128)(2,1)}, bf16[448,2,1152]{2,1,0:T(2,128)(2,1)}, u32[]{:S(2)}, u32[]{:S(2)}) collective-permute-start(bf16[448,2,1152]{2,1,0:T(2,128)(2,1)} %param.18), channel_id=1, source_target_pairs={{0,1},{1,0},{2,3},{3,2},{4,5},{5,4},{6,7},{7,6},{8,9},{9,8},{10,11... | collective-permute-start | bytes 6193160 | tf_op jit(solution)/shard_map/ppermute | solution.py:195
  0.0 16.6 %collective-permute-start.1 = (bf16[448,1024]{1,0:T(8,128)(2,1)}, bf16[448,1024]{1,0:T(8,128)(2,1)S(1)}, u32[]{:S(2)}, u32[]{:S(2)}) collective-permute-start(bf16[448,1024]{1,0:T(8,128)(2,1)} %bitcast.31), channel_id=1, source_target_pairs={{0,1},{1,0},{2,3},{3,2},{4,5},{5,4},{6,7},{7,6},{8,9},{9,8},{10,11... | collective-permute-start | bytes 2752520 | tf_op jit(solution)/shard_map/ppermute | solution.py:195
  0.5 17.1 %collective-permute-start.3 = (bf16[448,1152]{1,0:T(8,128)(2,1)}, bf16[448,1152]{1,0:T(8,128)(2,1)}, u32[]{:S(2)}, u32[]{:S(2)}) collective-permute-start(bf16[448,1152]{1,0:T(8,128)(2,1)} %bitcast.29), channel_id=1, source_target_pairs={{0,1},{1,0},{2,3},{3,2},{4,5},{5,4},{6,7},{7,6},{8,9},{9,8},{10,11... | collective-permute-start | bytes 3096584 | tf_op jit(solution)/shard_map/ppermute | solution.py:195
  0.6 25.0 %collective-permute-start = (bf16[8,512,128]{2,1,0:T(8,128)(2,1)}, bf16[8,512,128]{2,1,0:T(8,128)(2,1)}, u32[]{:S(2)}, u32[]{:S(2)}) collective-permute-start(bf16[8,512,128]{2,1,0:T(8,128)(2,1)} %own_ref.1), channel_id=1, source_target_pairs={{0,1},{1,0},{2,3},{3,2},{4,5},{5,4},{6,7},{7,6},{8,9},{9,8},{10,11... | collective-permute-start | bytes 3145736 | tf_op jit(solution)/shard_map/ppermute | solution.py:195
  4.8 20.7 %all-to-all-start = ((bf16[8,2,16,512]{3,2,1,0:T(8,128)(2,1)}), bf16[8,2,16,512]{3,2,1,0:T(8,128)(2,1)}, u32[]{:S(2)}, u32[]{:S(2)}) async-start(bf16[8,2,16,512]{3,2,1,0:T(8,128)(2,1)} %shard_map.100), calls=%async_computation | async-start | bytes 524288 | tf_op jit(solution)/shard_map/all_to_all | solution.py:23
  14.1 1.9 %copy-start.8 = (bf16[448]{0:T(512)(128)(2,1)S(1)}, bf16[448]{0:T(512)(128)(2,1)}, u32[]{:S(2)}) copy-start(bf16[448]{0:T(512)(128)(2,1)} %param.17) | copy-start | bytes 2692
  25.6 1.2 copy-start.3
  26.8 24.2 %copy-start.2 = (bf16[448,1024]{1,0:T(8,128)(2,1)S(1)}, bf16[448,1024]{1,0:T(8,128)(2,1)}, u32[]{:S(2)}) copy-start(bf16[448,1024]{1,0:T(8,128)(2,1)} %broadcast_multiply_fusion.1.other_ref) | copy-start | bytes 2752516
  26.8 24.2 %copy-start.5 = (bf16[1024,448]{0,1:T(8,128)(2,1)S(1)}, bf16[1024,448]{0,1:T(8,128)(2,1)}, u32[]{:S(2)}) copy-start(bf16[1024,448]{0,1:T(8,128)(2,1)} %param.16) | copy-start | bytes 2752516
  51.0 16.4 %copy-start.6 = (bf16[32,448]{1,0:T(8,128)(2,1)S(1)}, bf16[32,448]{1,0:T(8,128)(2,1)}, u32[]{:S(2)}) copy-start(bf16[32,448]{1,0:T(8,128)(2,1)} %copy.12.mine_ref) | copy-start | bytes 86020
  51.0 16.4 %copy-start.7 = (bf16[1,448]{1,0:T(2,128)(2,1)S(1)}, bf16[1,448]{1,0:T(2,128)(2,1)}, u32[]{:S(2)}) copy-start(bf16[1,448]{1,0:T(2,128)(2,1)} %reshape.46.gain_ref) | copy-start | bytes 2692
  51.8 31.6 %copy-start.1 = (bf16[56,8,2,1152]{3,1,2,0:T(8,128)(2,1)S(1)}, bf16[56,8,2,1152]{3,1,2,0:T(8,128)(2,1)}, u32[]{:S(2)}) copy-start(bf16[56,8,2,1152]{3,1,2,0:T(8,128)(2,1)} %copy.14) | copy-start | bytes 6193156
  116.8 20.5 %copy-start.4 = (bf16[1152,448]{0,1:T(8,128)(2,1)S(1)}, bf16[1152,448]{0,1:T(8,128)(2,1)}, u32[]{:S(2)}) copy-start(bf16[1152,448]{0,1:T(8,128)(2,1)} %param.19) | copy-start | bytes 3096580
